TPU v7x, 32 devices: a whole 2x2x4 slice. The times are simulated.
32 devices in a mesh: groups: 2 (over y), row: 4 (over z), col: 2 (over x), dp: 2 (over core).
Axes of the slice: x: 2, y: 2, z: 4, core: 2. Of those that a mesh axis runs over, the one named last changes fastest.
Arguments:
- tokens: bfloat16 [64, 6144], P(('groups', 'dp', 'row'), 'col'), parts along dimension 0, may hold values from -6 to 6
- cotangent: bfloat16 [64, 6144], P(('groups', 'dp', 'row'), 'col'), parts along dimension 0, may hold values from -6 to 6
- up_blocks: bfloat16 [4, 2, 576, 128, 128], P('row', 'col'), may hold values from -0.109375 to 0.109375
- down_blocks: bfloat16 [4, 2, 576, 128, 128], P('row', 'col'), may hold values from -0.0546875 to 0.0546875
- up_index: int32 [4, 2, 576, 2], P('row', 'col'), may hold values from 0 to 47, as said below
- down_index: int32 [4, 2, 576, 2], P('row', 'col'), may hold values from 0 to 47, as said below
- tile_counts: int32 [4, 2, 2], P('row', 'col'), may hold values from 432 to 576, as said below
- up_cover_rows: float32 [6144], P('col'), may hold values from 10 to 1000
- up_cover_cols: float32 [24576], P('row'), may hold values from 10 to 1000
- down_cover_rows: float32 [24576], P('row'), may hold values from 10 to 1000
- down_cover_cols: float32 [6144], P('col'), may hold values from 10 to 1000
Outputs:
- mixed: bfloat16 [64, 6144], P(('groups', 'dp', 'row'), 'col'), parts along dimension 0
- token_grad: bfloat16 [64, 6144], P(('groups', 'dp', 'row'), 'col'), parts along dimension 0
- up_step: bfloat16 [8, 2, 576, 128, 128], P(('groups', 'row'), 'col', 'dp'), parts along dimension 0
- down_step: bfloat16 [8, 2, 576, 128, 128], P(('groups', 'row'), 'col', 'dp'), parts along dimension 0
- up_rows_new: float32 [12288], P(('groups', 'col')), parts along dimension 0
- up_cols_new: float32 [49152], P(('groups', 'row')), parts along dimension 0
- down_rows_new: float32 [49152], P(('groups', 'row')), parts along dimension 0
- down_cols_new: float32 [12288], P(('groups', 'col')), parts along dimension 0
There are 2 independent parts, one for each index of `groups`. A program takes and returns all parts, laid end to end along the dimension named above; an argument that names none is the same for every part. Nothing has to cross between parts.
Inputs may be any that keep to these rules, and one draw needn't show every extreme that they name: `up_index`: each tile's 576 slots name distinct blocks of its 24 x 48 blocks: entry 0 is the feature block (below 24), entry 1 the hidden-unit block (below 48). `down_index`: as for up_index, drawn independently. `tile_counts`: some tile is full in each weight.
All inputs are finite; a program needn't handle non-finite values.
Results may differ from a plain program's by a relative error of at most 0.015.
Values may be sent and summed in bfloat16 or wider, within the bound.
A program may use at most 384 MiB of HBM per device.

v0:
```python
import jax
import jax.numpy as jnp
from jax import lax
from jax.sharding import PartitionSpec as P

precise = lax.Precision.HIGHEST


def silu_pair(hidden_pre):
    sigmoid_val = 1.0 / (1.0 + jnp.exp(-hidden_pre))
    return (hidden_pre * sigmoid_val, sigmoid_val * (1.0 + hidden_pre * (1.0 - sigmoid_val)))


def slot_map(positions, live_count, places):
    slot_ids = jnp.arange(positions.shape[0], dtype=jnp.int32)
    place_ids = jnp.arange(places, dtype=jnp.int32)
    matched = (positions[:, None] == place_ids[None, :]) & (slot_ids < live_count)[:, None]
    return matched.astype(jnp.float32)


def scatter_max(values, positions, places):
    matched = positions[:, None] == jnp.arange(places, dtype=jnp.int32)[None, :]
    return jnp.max(jnp.where(matched[:, :, None], values[:, None, :], 0.0), axis=0).reshape(-1)


def precondition(gradient, row_pos, col_pos, live_mask, row_cover, col_cover):
    width_block = gradient.shape[-1]
    row_side = jnp.take(row_cover.reshape(-1, width_block), row_pos, axis=0)
    col_side = jnp.take(col_cover.reshape(-1, width_block), col_pos, axis=0)
    second = jnp.minimum(row_side[:, :, None], col_side[:, None, :]) + gradient * gradient
    live_cube = live_mask[:, None, None]
    scaled = jnp.where(live_cube, gradient / jnp.sqrt(second), 0.0)
    largest = jnp.where(live_cube, second, 0.0)
    row_best = scatter_max(jnp.max(largest, axis=2), row_pos, row_cover.shape[0] // width_block)
    col_best = scatter_max(jnp.max(largest, axis=1), col_pos, col_cover.shape[0] // width_block)
    return (
        scaled.astype(jnp.bfloat16),
        jnp.maximum(row_cover, row_best),
        jnp.maximum(col_cover, col_best),
    )


def block_product(source, blocks, take_pos, spread, pattern):
    token_count = source.shape[0]
    width_block = blocks.shape[-1]
    picked = jnp.take(source.reshape(token_count, -1, width_block), take_pos, axis=1)
    product = jnp.einsum(pattern, picked, blocks, preferred_element_type=jnp.float32)
    placed = jnp.einsum("tsk,sm->tmk", product, spread, precision=precise)
    return placed.reshape(token_count, -1)


def on_device(
    tokens,
    cotangent,
    up_blocks,
    down_blocks,
    up_index,
    down_index,
    tile_counts,
    up_cover_rows,
    up_cover_cols,
    down_cover_rows,
    down_cover_cols,
):
    up_weight = up_blocks[0, 0]
    down_weight = down_blocks[0, 0]
    up_slots = up_index[0, 0]
    down_slots = down_index[0, 0]
    up_live_count = tile_counts[0, 0, 0]
    down_live_count = tile_counts[0, 0, 1]
    width_block = up_weight.shape[-1]
    feature_blocks = tokens.shape[1] // width_block
    unit_blocks = up_cover_cols.shape[0] // width_block
    up_to_units = slot_map(up_slots[:, 1], up_live_count, unit_blocks)
    up_to_features = slot_map(up_slots[:, 0], up_live_count, feature_blocks)
    down_to_units = slot_map(down_slots[:, 1], down_live_count, unit_blocks)
    down_to_features = slot_map(down_slots[:, 0], down_live_count, feature_blocks)
    gathered = lax.all_gather(tokens, "row", axis=0, tiled=True)
    group_tokens = gathered.shape[0]
    partial_hidden = block_product(gathered, up_weight, up_slots[:, 0], up_to_units, "tsp,spq->tsq")
    hidden_full = lax.psum(partial_hidden.astype(jnp.bfloat16), "col").astype(jnp.float32)
    act_full, slope_full = silu_pair(hidden_full)
    activation = act_full.astype(jnp.bfloat16)
    act_block = activation
    mixed = lax.psum_scatter(
        block_product(
            act_block, down_weight, down_slots[:, 1], down_to_features, "tsq,sqp->tsp"
        ).astype(jnp.bfloat16),
        "row",
        scatter_dimension=0,
        tiled=True,
    )
    act_picked = jnp.take(
        activation.reshape(group_tokens, unit_blocks, width_block), down_slots[:, 1], axis=1
    )
    cot_piece = lax.all_gather(cotangent, "row", axis=0, tiled=True)
    piece_rows = cot_piece.shape[0]
    picked = jnp.take(
        cot_piece.reshape(piece_rows, feature_blocks, width_block), down_slots[:, 0], axis=1
    )
    product = jnp.einsum("tsp,sqp->tsq", picked, down_weight, preferred_element_type=jnp.float32)
    placed = jnp.einsum("tsk,sm->tmk", product, down_to_units, precision=precise).reshape(
        piece_rows, -1
    )
    dact_part = placed
    act_block = act_picked
    down_grad = jnp.einsum("tsq,tsp->sqp", act_block, picked, preferred_element_type=jnp.float32)
    dact_part, down_grad = (dact_part, down_grad)
    dact_full = lax.psum(dact_part.astype(jnp.bfloat16), "col").astype(jnp.float32)
    dhidden = (dact_full * slope_full).astype(jnp.bfloat16)
    token_grad = lax.psum_scatter(
        block_product(dhidden, up_weight, up_slots[:, 1], up_to_features, "tsq,spq->tsp").astype(
            jnp.bfloat16
        ),
        "row",
        scatter_dimension=0,
        tiled=True,
    )
    token_picked = jnp.take(
        gathered.reshape(group_tokens, feature_blocks, width_block), up_slots[:, 0], axis=1
    )
    unit_picked = jnp.take(
        dhidden.reshape(group_tokens, unit_blocks, width_block), up_slots[:, 1], axis=1
    )
    up_grad = jnp.einsum(
        "tsp,tsq->spq", token_picked, unit_picked, preferred_element_type=jnp.float32
    )
    slot_total = up_weight.shape[0]
    half_slots = slot_total // lax.axis_size("dp")
    first_slot = lax.axis_index("dp") * half_slots
    up_sum, down_sum = (
        lax.psum(up_grad.astype(jnp.bfloat16), "dp").astype(jnp.float32),
        lax.psum(down_grad.astype(jnp.bfloat16), "dp").astype(jnp.float32),
    )
    slot_ids = jnp.arange(slot_total, dtype=jnp.int32)
    up_every, up_rows_local, up_cols_local = precondition(
        up_sum,
        up_slots[:, 0],
        up_slots[:, 1],
        slot_ids < up_live_count,
        up_cover_rows,
        up_cover_cols,
    )
    down_every, down_rows_local, down_cols_local = precondition(
        down_sum,
        down_slots[:, 1],
        down_slots[:, 0],
        slot_ids < down_live_count,
        down_cover_rows,
        down_cover_cols,
    )
    up_step = lax.dynamic_slice_in_dim(up_every, first_slot, half_slots, 0)
    down_step = lax.dynamic_slice_in_dim(down_every, first_slot, half_slots, 0)
    up_rows_new, down_cols_new = lax.pmax((up_rows_local, down_cols_local), "row")
    up_cols_new, down_rows_new = lax.pmax((up_cols_local, down_rows_local), "col")
    return (
        mixed,
        token_grad,
        up_step[None, None],
        down_step[None, None],
        up_rows_new,
        up_cols_new,
        down_rows_new,
        down_cols_new,
    )


def solution(mesh):
    in_specs = (
        P(("groups", "dp", "row"), "col"),
        P(("groups", "dp", "row"), "col"),
        P("row", "col", None, None, None),
        P("row", "col", None, None, None),
        P("row", "col", None, None),
        P("row", "col", None, None),
        P("row", "col", None),
        P("col"),
        P("row"),
        P("row"),
        P("col"),
    )
    out_specs = (
        P(("groups", "dp", "row"), "col"),
        P(("groups", "dp", "row"), "col"),
        P(("groups", "row"), "col", "dp", None, None),
        P(("groups", "row"), "col", "dp", None, None),
        P(("groups", "col")),
        P(("groups", "row")),
        P(("groups", "row")),
        P(("groups", "col")),
    )
    return jax.shard_map(
        on_device, mesh=mesh, in_specs=in_specs, out_specs=out_specs, check_vma=False
    )
```

profile of v0, /device:TPU:0, one launch (start us, length us, event | category | flops | bytes accessed | tf_op | source)
XLA Modules:
  0.0 487.7 jit_solution(10922371966925926850)
XLA Ops:
  7.2 15.2 %all-gather = bf16[4,4,3072]{2,1,0:T(4,128)(2,1)S(1)} all-gather(bf16[1,4,3072]{2,1,0:T(4,128)(2,1)} %bitcast.133), channel_id=1, replica_groups=mesh['groups'=2,'row'=4,'col'=2,'dp'=2] {'row'}, dimensions={0}, use_global_device_ids=true | all-gather | bytes 122880 | tf_op jit(solution)/shard_map/all_gather | solution.py:78
  22.5 0.8 slice_reduce_fusion.1
  23.4 1.3 fusion.90
  24.7 0.6 iota_compare_fusion.4
  25.3 2.6 gather_fusion
  27.9 10.1 %fusion.30 = f32[16,576,128]{2,0,1:T(8,128)S(1)} fusion(bf16[1,1,576,128,128]{4,3,2,1,0:T(8,128)(2,1)} %param.21, bf16[576,16,128]{2,1,0:T(8,128)(2,1)S(1)} %gather_fusion, pred[576]{0:T(1024)(128)(4,1)S(1)} %get-tuple-element.37), kind=kOutput, calls=%fused_computation.58 | convolution fusion | flops 303169536 | bytes 25952832 | tf_op jit(solution)/shard_map/tsp,spq->tsq/dot_general | solution.py:47
  38.0 3.1 fusion.50
  41.2 0.7 copy.92
  41.9 13.6 %all-gather.1 = bf16[4,4,3072]{2,1,0:T(4,128)(2,1)S(1)} all-gather(bf16[1,4,3072]{2,1,0:T(4,128)(2,1)S(1)} %bitcast.134), channel_id=1, replica_groups=mesh['groups'=2,'row'=4,'col'=2,'dp'=2] {'row'}, dimensions={0}, use_global_device_ids=true | all-gather | bytes 122880 | tf_op jit(solution)/shard_map/all_gather | solution.py:96
  55.7 0.7 iota_compare_fusion.5
  56.4 2.6 gather_fusion.2
  59.0 13.1 %fusion.45 = f32[16,576,128]{2,0,1:T(8,128)S(1)} fusion(bf16[1,1,576,128,128]{4,3,2,1,0:T(8,128)(2,1)} %param.22, bf16[576,16,128]{2,1,0:T(8,128)(2,1)S(1)} %gather_fusion.2, pred[576]{0:T(1024)(128)(4,1)S(1)} %get-tuple-element.38), kind=kOutput, calls=%fused_computation.61 | convolution fusion | flops 303169536 | bytes 25952832 | tf_op jit(solution)/shard_map/tsp,sqp->tsq/dot_general | solution.py:101
  72.0 3.2 fusion.53
  75.2 0.7 copy.91
  76.3 26.6 %all-reduce.15.cloned.1.call-done = (bf16[16,6144]{1,0:T(8,128)(2,1)}, bf16[16,6144]{1,0:T(8,128)(2,1)}) async-done(((bf16[16,6144]{1,0:T(8,128)(2,1)}, bf16[16,6144]{1,0:T(8,128)(2,1)}), (bf16[16,6144]{1,0:T(8,128)(2,1)}, bf16[16,6144]{1,0:T(8,128)(2,1)})) %all-reduce.15.cloned.1.call-update) | async-done | bytes 393232 | tf_op jit(solution)/shard_map/psum | solution.py:81
  102.9 1.2 fusion.71
  104.2 3.2 gather_fusion.3
  107.4 15.7 %fusion.35 = f32[16,576,128]{2,0,1:T(8,128)} fusion(bf16[1,1,576,128,128]{4,3,2,1,0:T(8,128)(2,1)} %param.21, bf16[576,16,128]{2,1,0:T(8,128)(2,1)} %gather_fusion.3, pred[576]{0:T(1024)(128)(4,1)S(1)} %get-tuple-element.36), kind=kOutput, calls=%fused_computation.59 | convolution fusion | flops 303169536 | bytes 25952832 | tf_op jit(solution)/shard_map/tsq,spq->tsp/dot_general | solution.py:47
  123.2 11.2 %convolution_convert_fusion.1 = bf16[576,128,128]{2,1,0:T(8,128)(2,1)} fusion(bf16[576,16,128]{2,1,0:T(8,128)(2,1)S(1)} %copy-done.7, pred[576]{0:T(1024)(128)(4,1)S(1)} %get-tuple-element.37, bf16[576,16,128]{2,1,0:T(8,128)(2,1)S(1)} %copy-done.5, pred[576]{0:T(1024)(128)(4,1)S(1)} %get-tuple-element.36), kind=kOutput, calls=%fused_computation.33 | convolution fusion | flops 313786368 | bytes 23594112 | tf_op jit(solution)/shard_map/tsp,tsq->spq/dot_general | solution.py:125
  134.4 3.2 gather_fusion.1
  137.7 10.0 %fusion.40 = f32[16,576,128]{2,0,1:T(8,128)S(1)} fusion(bf16[1,1,576,128,128]{4,3,2,1,0:T(8,128)(2,1)} %param.22, bf16[576,16,128]{2,1,0:T(8,128)(2,1)} %gather_fusion.1, pred[576]{0:T(1024)(128)(4,1)S(1)} %get-tuple-element.39), kind=kOutput, calls=%fused_computation.60 | convolution fusion | flops 303169536 | bytes 25952832 | tf_op jit(solution)/shard_map/tsq,sqp->tsp/dot_general | solution.py:47
  147.6 2.9 fusion.56
  150.5 0.7 copy.96
  151.2 5.1 %fusion.59 = bf16[24,16,128]{2,0,1:T(8,128)(2,1)S(1)} fusion(f32[16,576,128]{2,0,1:T(8,128)} %fusion.35, pred[576]{0:T(1024)(128)(4,1)S(1)} %iota_compare_fusion.4, s32[576]{0:T(1024)S(1)} %get-tuple-element.19), kind=kOutput, calls=%fused_computation.65 | convolution fusion | flops 339815424 | bytes 4819776 | tf_op jit(solution)/shard_map/tsk,sm->tmk/dot_general | solution.py:48
  156.3 0.7 copy.95
  157.1 13.4 %convolution_convert_fusion = bf16[576,128,128]{2,1,0:T(8,128)(2,1)} fusion(bf16[576,16,128]{2,1,0:T(8,128)(2,1)} %gather_fusion.1, pred[576]{0:T(1024)(128)(4,1)S(1)} %get-tuple-element.39, bf16[576,16,128]{2,1,0:T(8,128)(2,1)S(1)} %gather_fusion.2, pred[576]{0:T(1024)(128)(4,1)S(1)} %get-tuple-element.38), kind=kOutput, calls=%fused_computation.32 | convolution fusion | flops 313786368 | bytes 23594112 | tf_op jit(solution)/shard_map/tsq,tsp->sqp/dot_general | solution.py:107
  171.2 1.6 gather_fusion.5
  172.9 1.6 gather_fusion.4
  174.5 1.6 gather_fusion.7
  176.1 1.6 gather_fusion.6
  178.7 0.6 dynamic-slice
  180.5 11.6 %all-reduce.11.cloned.1.call-done = (bf16[16,3072]{1,0:T(8,128)(2,1)}, bf16[16,3072]{1,0:T(8,128)(2,1)}) async-done(((bf16[16,3072]{1,0:T(8,128)(2,1)}, bf16[16,3072]{1,0:T(8,128)(2,1)}), (bf16[16,3072]{1,0:T(8,128)(2,1)}, bf16[16,3072]{1,0:T(8,128)(2,1)})) %all-reduce.11.cloned.1.call-update) | async-done | bytes 196624
  192.1 1.4 constant_dynamic-slice_fusion.1
  193.6 1.4 constant_dynamic-slice_fusion
  195.0 112.2 %all-reduce.13.cloned.1.call-done = (bf16[576,128,128]{2,1,0:T(8,128)(2,1)}, bf16[576,128,128]{2,1,0:T(8,128)(2,1)}) async-done(((bf16[576,128,128]{2,1,0:T(8,128)(2,1)}, bf16[576,128,128]{2,1,0:T(8,128)(2,1)}), (bf16[576,128,128]{2,1,0:T(8,128)(2,1)}, bf16[576,128,128]{2,1,0:T(8,128)(2,1)})) %all-reduce.13.cloned.1.call-update) | async-done | bytes 37748752 | tf_op jit(solution)/shard_map/psum | solution.py:132
  307.1 21.3 %convert_element_type.87 = f32[576,128,128]{2,1,0:T(8,128)} convert(bf16[576,128,128]{2,1,0:T(8,128)(2,1)} %get-tuple-element.26) | non-fusion elementwise | flops 9437184 | bytes 56623104 | tf_op jit(solution)/shard_map/convert_element_type | solution.py:132
  328.5 4.1 copy-done.4
  332.6 12.5 %convert_element_type.90 = f32[576,128,128]{2,1,0:T(8,128)} convert(bf16[576,128,128]{2,1,0:T(8,128)(2,1)S(1)} %copy-done.4) | non-fusion elementwise | flops 9437184 | bytes 56623104 | tf_op jit(solution)/shard_map/convert_element_type | solution.py:133
  345.1 30.1 %select_reduce_fusion.2 = (f32[576,128]{1,0:T(8,128)S(1)}, f32[576,128]{1,0:T(8,128)S(1)}, f32[576,128,128]{2,1,0:T(8,128)}) fusion(pred[576]{0:T(1024)(128)(4,1)S(1)} %iota_compare_fusion.4, bf16[576,128,128]{2,1,0:T(8,128)(2,1)} %get-tuple-element.26, f32[576,128]{1,0:T(8,128)S(1)} %broadcast_select_fusion.14, f32[576,128]{1,0:T(8,128)S(1)} %broadcast_select_fusion.15), kind=kLoop, calls=%fused_computation.12 | loop fusion | flops 65912832 | bytes 57803328 | tf_op jit(solution)/shard_map/reduce_max | solution.py:35
  375.2 2.5 select_reduce_fusion.7
  377.7 27.0 %select_reduce_fusion = (f32[576,128]{1,0:T(8,128)S(1)}, f32[576,128]{1,0:T(8,128)S(1)}, f32[576,128,128]{2,1,0:T(8,128)}) fusion(pred[576]{0:T(1024)(128)(4,1)S(1)} %iota_compare_fusion.5, bf16[576,128,128]{2,1,0:T(8,128)(2,1)S(1)} %copy-done.4, f32[576,128]{1,0:T(8,128)S(1)} %broadcast_select_fusion.12, f32[576,128]{1,0:T(8,128)S(1)} %broadcast_select_fusion.13), kind=kLoop, calls=%fused_computation.10 | loop fusion | flops 65912832 | bytes 57803328 | tf_op jit(solution)/shard_map/reduce_max | solution.py:35
  404.7 2.5 select_reduce_fusion.6
  407.2 5.1 %select_reduce_fusion.5 = f32[48,128]{1,0:T(8,128)S(1)} fusion(f32[576,128]{1,0:T(8,128)S(1)} %get-tuple-element.14, pred[576,48]{1,0:T(8,128)(4,1)S(1)} %copy.60), kind=kLoop, calls=%fused_computation.31 | loop fusion | flops 7071744 | bytes 347136 | tf_op jit(solution)/shard_map/reduce_max | solution.py:23
  412.3 5.1 %select_reduce_fusion.4 = f32[48,128]{1,0:T(8,128)S(1)} fusion(f32[576,128]{1,0:T(8,128)S(1)} %get-tuple-element.13, pred[576,48]{1,0:T(8,128)(4,1)S(1)} %copy.61), kind=kLoop, calls=%fused_computation.30 | loop fusion | flops 7071744 | bytes 347136 | tf_op jit(solution)/shard_map/reduce_max | solution.py:23
  417.3 19.9 %all-reduce.2 = (f32[3072]{0:T(1024)}, f32[3072]{0:T(1024)}) all-reduce(f32[3072]{0:T(1024)S(1)} %bitcast_maximum_fusion.3, f32[3072]{0:T(1024)S(1)} %bitcast_maximum_fusion.2), channel_id=1, replica_groups=mesh['groups'=2,'row'=4,'col'=2,'dp'=2] {'row'}, use_global_device_ids=true, to_apply=%region_8.13 | all-reduce | flops 6144 | bytes 49152 | tf_op jit(solution)/shard_map/pmax | solution.py:154
  437.2 9.2 %all-reduce.3 = (f32[6144]{0:T(1024)}, f32[6144]{0:T(1024)}) all-reduce(f32[6144]{0:T(1024)S(1)} %bitcast_maximum_fusion.1, f32[6144]{0:T(1024)S(1)} %bitcast_maximum_fusion), channel_id=1, replica_groups=mesh['groups'=2,'row'=4,'col'=2,'dp'=2] {'col'}, use_global_device_ids=true, to_apply=%region_11.16 | all-reduce | flops 12288 | bytes 98304 | tf_op jit(solution)/shard_map/pmax | solution.py:155
  446.4 17.2 %fusion.12 = bf16[1,1,288,128,128]{4,3,2,1,0:T(8,128)(2,1)} fusion(f32[576,128,128]{2,1,0:T(8,128)} %get-tuple-element.31, s32[]{:T(128)S(6)} %select_n.57, f32[576,128,128]{2,1,0:T(8,128)} %convert_element_type.87, pred[288]{0:T(512)(128)(4,1)S(1)} %dynamic-slice.4), kind=kLoop, calls=%fused_computation.34 | loop fusion | flops 14155776 | bytes 47186212 | tf_op jit(solution)/shard_map/broadcast_in_dim | solution.py:159
  463.6 17.2 %fusion.13 = bf16[1,1,288,128,128]{4,3,2,1,0:T(8,128)(2,1)} fusion(f32[576,128,128]{2,1,0:T(8,128)} %get-tuple-element.30, s32[]{:T(128)S(6)} %select_n.57, f32[576,128,128]{2,1,0:T(8,128)} %convert_element_type.90, pred[288]{0:T(512)(128)(4,1)S(1)} %dynamic-slice.5), kind=kLoop, calls=%fused_computation.35 | loop fusion | flops 14155776 | bytes 47186212 | tf_op jit(solution)/shard_map/broadcast_in_dim | solution.py:160
  (62 shorter events, 2.8 us)
Async XLA Ops:
  7.2 95.8 %all-reduce.15.cloned.1.call-start = ((), (), s32[]{:S(2)}) async-start(), calls=%async_computation.2 | async-start | bytes 786432 | tf_op jit(solution)/shard_map/psum | solution.py:81
  27.9 10.1 %copy-start.6 = (bf16[576,16,128]{2,1,0:T(8,128)(2,1)}, bf16[576,16,128]{2,1,0:T(8,128)(2,1)S(1)}, u32[]{:S(2)}) copy-start(bf16[576,16,128]{2,1,0:T(8,128)(2,1)S(1)} %gather_fusion) | copy-start | bytes 7077892
  38.0 3.9 copy-start.8
  38.0 17.6 %copy-start.9 = (s32[1,1,576,2]{2,3,1,0:T(2,128)S(1)}, s32[1,1,576,2]{2,3,1,0:T(2,128)}, u32[]{:S(2)}) copy-start(s32[1,1,576,2]{2,3,1,0:T(2,128)} %param.24) | copy-start | bytes 13828
  76.0 116.2 %all-reduce.11.cloned.1.call-start = ((), (), s32[]{:S(2)}) async-start(), calls=%async_computation | async-start | bytes 393216
  107.4 15.7 %copy-start.5 = (bf16[576,16,128]{2,1,0:T(8,128)(2,1)S(1)}, bf16[576,16,128]{2,1,0:T(8,128)(2,1)}, u32[]{:S(2)}) copy-start(bf16[576,16,128]{2,1,0:T(8,128)(2,1)} %gather_fusion.3) | copy-start | bytes 7077892
  107.4 15.7 %copy-start.7 = (bf16[576,16,128]{2,1,0:T(8,128)(2,1)S(1)}, bf16[576,16,128]{2,1,0:T(8,128)(2,1)}, u32[]{:S(2)}) copy-start(bf16[576,16,128]{2,1,0:T(8,128)(2,1)} %copy-done.6) | copy-start | bytes 7077892
  157.0 150.1 %all-reduce.13.cloned.1.call-start = ((), (), s32[]{:S(2)}) async-start(), calls=%async_computation.1 | async-start | bytes 75497472 | tf_op jit(solution)/shard_map/psum | solution.py:132
  170.5 0.7 copy-start.2
  170.5 2.4 copy-start
  170.5 4.0 copy-start.1
  170.5 5.6 %copy-start.3 = (f32[6144]{0:T(1024)S(1)}, f32[6144]{0:T(1024)}, u32[]{:S(2)}) copy-start(f32[6144]{0:T(1024)} %param.28) | copy-start | bytes 73732
  172.8 5.8 %copy-start.10 = (u32[32]{0:T(128)S(1)}, u32[32]{0:T(128)}, u32[]{:S(2)}) copy-start(u32[32]{0:T(128)} %constant.65) | copy-start | bytes 388
  307.1 25.4 %copy-start.4 = (bf16[576,128,128]{2,1,0:T(8,128)(2,1)S(1)}, bf16[576,128,128]{2,1,0:T(8,128)(2,1)}, u32[]{:S(2)}) copy-start(bf16[576,128,128]{2,1,0:T(8,128)(2,1)} %get-tuple-element.27) | copy-start | bytes 56623108
Sparse Core Ops, SparseCore 0:
  76.1 26.7 all-reduce.14
  157.1 34.9 all-reduce.10
  194.7 112.3 all-reduce.12
where the time goes:
time: 493 us; the launch traced here: 488 us
  waiting for transfers between devices  150 us (30%)
  other arithmetic  144 us (29%)
  matrix products  87.8 us (18%)
  blocking collectives  57.9 us (12%)
  local copies, waits for them, and re-layouts  32.2 us (7%)
  between operations  15.3 us (3%)
    psum x1, waiting for transfers between devices, on_device(): lax.psum(up_grad.astype(jnp.bfloat16), 'dp').astype(jnp.float32)  112 us
    reduce_max x2, other arithmetic, precondition(): jnp.max(largest, axis=1)  57.1 us
    dot_general x3, matrix products, block_product(): jnp.einsum(pattern, picked, blocks, preferred_element_type=jnp.float32)  35.8 us
    psum x1, waiting for transfers between devices, on_device(): lax.psum(partial_hidden.astype(jnp.bfloat16), 'col').astype(jnp.float32)  26.6 us
    convert_element_type x1, other arithmetic, on_device(): lax.psum(up_grad.astype(jnp.bfloat16), 'dp').astype(jnp.float32)  21.3 us
    pmax x1, blocking collectives, on_device(): lax.pmax((up_rows_local, down_cols_local), 'row')  19.9 us
    broadcast_in_dim x1, other arithmetic, on_device(): up_step[None, None]  17.2 us
    broadcast_in_dim x1, other arithmetic, on_device(): down_step[None, None]  17.2 us
  transfers between devices with their start and end apart: 3, of which 3 were waited for; matrix products, arithmetic and copies ran while one was open for 5% of the time, Pallas kernels for 0%

commit v1 on v0

v1 whole, which is shorter than its diff:
```python
import functools

import jax
import jax.numpy as jnp
from jax import lax
from jax.experimental import pallas as pl
from jax.experimental.pallas import tpu as pltpu
from jax.sharding import PartitionSpec as P

MESH = pl.DeviceIdType.MESH
VMEM_LIMIT = 56 * 1024 * 1024
NN = (((1,), (0,)), ((), ()))
NT = (((1,), (1,)), ((), ()))


def largest_divisor(total, most):
    return max(d for d in range(1, most + 1) if total % d == 0)


def dot(left, right, dims):
    return lax.dot_general(left, right, dims, preferred_element_type=jnp.float32)


def slot_places(index_ref, slot, live, features, units):
    alive = slot < live
    feature = jnp.where(alive, index_ref[2 * slot], features)
    unit = jnp.where(alive, index_ref[2 * slot + 1], units)
    return feature, unit


def first_kernel(
    chunk, batch, up_at, down_at, counts, place, x_ref, up_ref, down_ref, out_ref, hid, dac
):
    step = pl.program_id(0)
    features = x_ref.shape[1] - 1
    units = hid.shape[0] - 1
    shares, _, _, share_rows, _ = out_ref.shape

    @pl.when(step == 0)
    def _():
        hid[...] = jnp.zeros_like(hid)
        dac[...] = jnp.zeros_like(dac)

    first = place[0] * (chunk * pl.num_programs(0)) + step * chunk

    @pl.loop(0, chunk // batch)
    def _(part):
        work = []
        for j in range(batch):
            at = part * batch + j
            slot = first + at
            uf, uu = slot_places(up_at, slot, counts[0], features, units)
            df, du = slot_places(down_at, slot, counts[1], features, units)
            work.append((uu, dot(x_ref[0, uf], up_ref[at], NN), hid))
            work.append((du, dot(x_ref[1, df], down_ref[at], NT), dac))
        for unit, product, total in work:
            total[unit] += product

    @pl.when(step == pl.num_programs(0) - 1)
    def _():
        for share in range(shares):
            rows = pl.ds(share * share_rows, share_rows)
            out_ref[share, 0] = hid[:units, rows, :].astype(jnp.bfloat16)
            out_ref[share, 1] = dac[:units, rows, :].astype(jnp.bfloat16)


def first_products(up_at, down_at, counts, place, x, up_weight, down_weight, units, shares):
    slots = up_weight.shape[0] // shares
    _, features1, tokens, width = x.shape
    chunk = largest_divisor(slots, 24)
    batch = largest_divisor(chunk, 8)
    steps = slots // chunk
    weight = pl.BlockSpec(
        (chunk, width, width), lambda i, a, b, c, p: (p[0] * steps + i, 0, 0)
    )
    return pl.pallas_call(
        functools.partial(first_kernel, chunk, batch),
        grid_spec=pltpu.PrefetchScalarGridSpec(
            num_scalar_prefetch=4,
            grid=(steps,),
            in_specs=[
                pl.BlockSpec(x.shape, lambda i, a, b, c, p: (0, 0, 0, 0)),
                weight,
                weight,
            ],
            out_specs=pl.BlockSpec(
                (shares, 2, units, tokens // shares, width), lambda i, a, b, c, p: (0, 0, 0, 0, 0)
            ),
            scratch_shapes=[
                pltpu.VMEM((units + 1, tokens, width), jnp.float32),
                pltpu.VMEM((units + 1, tokens, width), jnp.float32),
            ],
        ),
        out_shape=jax.ShapeDtypeStruct(
            (shares, 2, units, tokens // shares, width), jnp.bfloat16
        ),
        compiler_params=pltpu.CompilerParams(vmem_limit_bytes=VMEM_LIMIT),
        cost_estimate=pl.CostEstimate(
            flops=4 * slots * tokens * width * width,
            bytes_accessed=4 * slots * width * width,
            transcendentals=0,
        ),
    )(up_at, down_at, counts, place, x, up_weight, down_weight)


def second_kernel(
    chunk,
    batch,
    up_at,
    down_at,
    counts,
    place,
    x_ref,
    h_ref,
    up_ref,
    down_ref,
    f_cover,
    u_cover,
    up_step,
    down_step,
    sums_ref,
    f_new,
    u_new,
    x_turned,
    act_turned,
    dh,
    act,
    f_rows,
    u_rows,
    f_rows_max,
    u_rows_max,
    f_cols,
    u_cols,
    f_cols_max,
    u_cols_max,
    mix,
    tok,
):
    step = pl.program_id(0)
    features = x_ref.shape[1] - 1
    units = h_ref.shape[1]
    width = x_ref.shape[-1]
    groups = width // 8

    @pl.when(step == 0)
    def _():
        mix[...] = jnp.zeros_like(mix)
        tok[...] = jnp.zeros_like(tok)
        dh[units] = jnp.zeros_like(dh[units])
        act[units] = jnp.zeros_like(act[units])
        act_turned[units] = jnp.zeros_like(act_turned[units])
        x_turned[features] = jnp.zeros_like(x_turned[features])
        f_rows[features] = jnp.ones_like(f_rows[features])
        u_rows[units] = jnp.ones_like(u_rows[units])
        f_cols[features] = jnp.ones_like(f_cols[features])
        u_cols[units] = jnp.ones_like(u_cols[units])
        f_cols_max[...] = jnp.zeros_like(f_cols_max)
        u_cols_max[...] = jnp.zeros_like(u_cols_max)

        @pl.loop(0, features)
        def _(f):
            x_turned[f] = x_ref[0, f].astype(jnp.float32).T.astype(jnp.bfloat16)
            wide = jnp.broadcast_to(f_cover[0, pl.ds(f, 1)], (width, width)).T
            f_rows[f] = wide
            f_rows_max[f] = wide
            f_cols[f] = f_cover[1, pl.ds(f, 1)]

        @pl.loop(0, units)
        def _(u):
            act[u] = h_ref[0, u]
            dh[u] = h_ref[1, u]
            act_turned[u] = h_ref[0, u].astype(jnp.float32).T.astype(jnp.bfloat16)
            wide = jnp.broadcast_to(u_cover[1, pl.ds(u, 1)], (width, width)).T
            u_rows[u] = wide
            u_rows_max[u] = wide
            u_cols[u] = u_cover[0, pl.ds(u, 1)]

    first = place[0] * (chunk * pl.num_programs(0)) + step * chunk

    def one_step(grad, rows, cols, rows_max, cols_max, row, col, step_ref, at):
        second = jnp.minimum(rows[row], cols[col]) + grad * grad
        step_ref[0, 0, at] = (grad * lax.rsqrt(second)).astype(jnp.bfloat16)
        rows_max[row] = jnp.maximum(rows_max[row], second)
        best = jnp.max(second.reshape(groups, 8, width), axis=0)
        cols_max[col] = jnp.maximum(cols_max[col], best)

    @pl.loop(0, chunk // batch)
    def _(part):
        work = []
        for j in range(batch):
            at = part * batch + j
            slot = first + at
            uf, uu = slot_places(up_at, slot, counts[0], features, units)
            df, du = slot_places(down_at, slot, counts[1], features, units)
            work.append((uf, dot(dh[uu], up_ref[at], NT), tok))
            work.append((df, dot(act[du], down_ref[at], NN), mix))
        for feature, product, total in work:
            total[feature] += product
        for j in range(batch):
            at = part * batch + j
            slot = first + at
            uf, uu = slot_places(up_at, slot, counts[0], features, units)
            df, du = slot_places(down_at, slot, counts[1], features, units)
            up_grad = dot(x_turned[uf], dh[uu], NN)
            down_grad = dot(act_turned[du], x_ref[1, df], NN)
            one_step(up_grad, f_rows, u_cols, f_rows_max, u_cols_max, uf, uu, up_step, at)
            one_step(down_grad, u_rows, f_cols, u_rows_max, f_cols_max, du, df, down_step, at)

    @pl.when(step == pl.num_programs(0) - 1)
    def _():
        sums_ref[0] = mix[:features].astype(jnp.bfloat16)
        sums_ref[1] = tok[:features].astype(jnp.bfloat16)

        @pl.loop(0, features)
        def _(f):
            f_new[0, pl.ds(f, 1)] = jnp.max(f_rows_max[f].T, axis=0, keepdims=True)
            best = jnp.max(f_cols_max[f], axis=0, keepdims=True)
            f_new[1, pl.ds(f, 1)] = jnp.maximum(best, f_cols[f])

        @pl.loop(0, units)
        def _(u):
            u_new[1, pl.ds(u, 1)] = jnp.max(u_rows_max[u].T, axis=0, keepdims=True)
            best = jnp.max(u_cols_max[u], axis=0, keepdims=True)
            u_new[0, pl.ds(u, 1)] = jnp.maximum(best, u_cols[u])


def second_products(
    up_at, down_at, counts, place, x, h, up_weight, down_weight, f_cover, u_cover, shares
):
    slots = up_weight.shape[0] // shares
    _, features1, tokens, width = x.shape
    features = features1 - 1
    units = h.shape[1]
    chunk = largest_divisor(slots, 24)
    batch = largest_divisor(chunk, 4)
    steps = slots // chunk
    weight = pl.BlockSpec(
        (chunk, width, width), lambda i, a, b, c, p: (p[0] * steps + i, 0, 0)
    )
    stepped = pl.BlockSpec(
        (1, 1, chunk, width, width), lambda i, a, b, c, p: (0, 0, i, 0, 0)
    )

    def whole(shape):
        return pl.BlockSpec(shape, lambda i, a, b, c, p: (0,) * len(shape))

    f32, bf16 = jnp.float32, jnp.bfloat16
    sums = (2, features, tokens, width)
    return pl.pallas_call(
        functools.partial(second_kernel, chunk, batch),
        grid_spec=pltpu.PrefetchScalarGridSpec(
            num_scalar_prefetch=4,
            grid=(steps,),
            in_specs=[
                whole(x.shape),
                whole(h.shape),
                weight,
                weight,
                whole(f_cover.shape),
                whole(u_cover.shape),
            ],
            out_specs=[stepped, stepped, whole(sums), whole(f_cover.shape), whole(u_cover.shape)],
            scratch_shapes=[
                pltpu.VMEM((features + 1, width, tokens), bf16),
                pltpu.VMEM((units + 1, width, tokens), bf16),
                pltpu.VMEM((units + 1, tokens, width), bf16),
                pltpu.VMEM((units + 1, tokens, width), bf16),
                pltpu.VMEM((features + 1, width, width), f32),
                pltpu.VMEM((units + 1, width, width), f32),
                pltpu.VMEM((features + 1, width, width), f32),
                pltpu.VMEM((units + 1, width, width), f32),
                pltpu.VMEM((features + 1, 1, width), f32),
                pltpu.VMEM((units + 1, 1, width), f32),
                pltpu.VMEM((features + 1, 8, width), f32),
                pltpu.VMEM((units + 1, 8, width), f32),
                pltpu.VMEM((features + 1, tokens, width), f32),
                pltpu.VMEM((features + 1, tokens, width), f32),
            ],
        ),
        out_shape=[
            jax.ShapeDtypeStruct((1, 1, slots, width, width), bf16),
            jax.ShapeDtypeStruct((1, 1, slots, width, width), bf16),
            jax.ShapeDtypeStruct(sums, bf16),
            jax.ShapeDtypeStruct(f_cover.shape, f32),
            jax.ShapeDtypeStruct(u_cover.shape, f32),
        ],
        compiler_params=pltpu.CompilerParams(vmem_limit_bytes=VMEM_LIMIT),
        cost_estimate=pl.CostEstimate(
            flops=8 * slots * tokens * width * width,
            bytes_accessed=8 * slots * width * width,
            transcendentals=2 * slots * width * width,
        ),
    )(up_at, down_at, counts, place, x, h, up_weight, down_weight, f_cover, u_cover)


def gather_inputs(own):
    return lax.all_gather(own, ("dp", "row"), axis=0, tiled=False)


def silu_pair(hidden):
    sigma = 1.0 / (1.0 + jnp.exp(-hidden))
    return hidden * sigma, sigma * (1.0 + hidden * (1.0 - sigma))


def hidden_exchange(partial):
    mine = lax.psum_scatter(partial, "dp", scatter_dimension=0, tiled=False)
    total = lax.psum(mine, "col").astype(jnp.float32)
    activation, slope = silu_pair(total[0])
    both = jnp.stack([activation, total[1] * slope]).astype(jnp.bfloat16)
    return lax.all_gather(both, "dp", axis=2, tiled=True)


def final_exchange(sums, f_new, u_new):
    own = lax.psum_scatter(sums, ("dp", "row"), scatter_dimension=0, tiled=False)
    return own, lax.pmax(f_new, ("row", "dp")), lax.pmax(u_new, ("col", "dp"))


def on_device(
    tokens,
    cotangent,
    up_blocks,
    down_blocks,
    up_index,
    down_index,
    tile_counts,
    up_cover_rows,
    up_cover_cols,
    down_cover_rows,
    down_cover_cols,
):
    width = up_blocks.shape[-1]
    own_tokens = tokens.shape[0]
    features = tokens.shape[1] // width
    units = up_cover_cols.shape[0] // width
    shares = lax.axis_size("dp")
    rows = lax.axis_size("row")
    all_tokens = own_tokens * rows * shares

    up_at = up_index.reshape(-1)
    down_at = down_index.reshape(-1)
    counts = tile_counts.reshape(-1)
    place = lax.axis_index("dp").astype(jnp.int32).reshape(1)
    up_weight = up_blocks.reshape(up_blocks.shape[2:])
    down_weight = down_blocks.reshape(down_blocks.shape[2:])

    own = jnp.stack([tokens, cotangent]).reshape(2 * own_tokens * features, width)
    gathered = gather_inputs(own).reshape(shares * rows, 2, own_tokens, features, width)
    x = gathered.transpose(1, 3, 0, 2, 4).reshape(2, features, all_tokens, width)
    x = jnp.pad(x, ((0, 0), (0, 1), (0, 0), (0, 0)))

    partial = first_products(
        up_at, down_at, counts, place, x, up_weight, down_weight, units, shares
    )
    h = hidden_exchange(partial)

    f_cover = jnp.stack([up_cover_rows, down_cover_cols]).reshape(2, features, width)
    u_cover = jnp.stack([up_cover_cols, down_cover_rows]).reshape(2, units, width)
    up_step, down_step, sums, f_new, u_new = second_products(
        up_at, down_at, counts, place, x, h, up_weight, down_weight, f_cover, u_cover, shares
    )
    sums = sums.reshape(2, features, shares * rows, own_tokens, width).transpose(2, 0, 3, 1, 4)
    sums = sums.reshape(shares * rows, 2 * own_tokens * features, width)
    out, f_new, u_new = final_exchange(sums, f_new, u_new)
    out = out.reshape(2, own_tokens, features * width)
    f_new = f_new.reshape(2, features * width)
    u_new = u_new.reshape(2, units * width)
    return (out[0], out[1], up_step, down_step, f_new[0], u_new[0], u_new[1], f_new[1])


def solution(mesh):
    in_specs = (
        P(("groups", "dp", "row"), "col"),
        P(("groups", "dp", "row"), "col"),
        P("row", "col", None, None, None),
        P("row", "col", None, None, None),
        P("row", "col", None, None),
        P("row", "col", None, None),
        P("row", "col", None),
        P("col"),
        P("row"),
        P("row"),
        P("col"),
    )
    out_specs = (
        P(("groups", "dp", "row"), "col"),
        P(("groups", "dp", "row"), "col"),
        P(("groups", "row"), "col", "dp", None, None),
        P(("groups", "row"), "col", "dp", None, None),
        P(("groups", "col")),
        P(("groups", "row")),
        P(("groups", "row")),
        P(("groups", "col")),
    )
    return jax.shard_map(
        on_device, mesh=mesh, in_specs=in_specs, out_specs=out_specs, check_vma=False
    )
```

time: 493 us -> 202 us (0.41)
  other arithmetic: 144 us -> 3.31 us
  waiting for transfers between devices: 150 us -> 37.6 us
  matrix products: 87.8 us -> 0 us
  Pallas kernels: 0 us -> 64.6 us
  local copies, waits for them, and re-layouts: 32.2 us -> 9.4 us
  blocking collectives: 57.9 us -> 72.1 us
    psum x2 -> x1, waiting for transfers between devices: 139 us -> 28 us  [hidden_exchange(): total = lax.psum(mine, 'col').astype(jnp.float32)]
    dot_general x10 -> x0, matrix products: 87.8 us -> none  [the longest x3 35.8 us: block_product(): jnp.einsum(pattern, picked, blocks, preferred_element_type=jnp.float32)]
    reduce_max x6 -> x0, other arithmetic: 72.2 us -> none  [the longest x2 57.1 us: precondition(): jnp.max(largest, axis=1)]
    pallas_call x0 -> x2, Pallas kernels: none -> 64.6 us  [the longest x1 46.8 us: second_products(): pl.pallas_call(functools.partial(second_kernel, chunk, batch), grid_spec=...]
    broadcast_in_dim x2 -> x0, other arithmetic: 34.4 us -> none  [the longest x1 17.2 us: on_device(): up_step[None, None]]
    convert_element_type x2 -> x1, other arithmetic: 33.9 us -> 1.05 us  [hidden_exchange(): total = lax.psum(mine, 'col').astype(jnp.float32)]
    gather x8 -> x0, local copies, waits for them, and re-layouts: 18.1 us -> none  [the longest x3 9.05 us: block_product(): jnp.take(source.reshape(token_count, -1, width_block), take_pos, axis=1)]
    pmax x2, blocking collectives: 29 us -> 42 us  [final_exchange(): return (own, lax.pmax(f_new, ('row', 'dp')), lax.pmax(u_new, ('col', 'dp')))]
  transfers between devices with their start and end apart: 3 -> 3, of which waited for: 3 -> 2; matrix products, arithmetic and copies ran while one was open for 5% -> 1% of each run, Pallas kernels for 0% -> 0%
where the time goes in v1:
time: 202 us; the launch traced here: 201 us
  blocking collectives  72.1 us (36%)
  Pallas kernels  64.6 us (32%)
  waiting for transfers between devices  37.6 us (19%)
  between operations  13.8 us (7%)
  local copies, waits for them, and re-layouts  9.4 us (5%)
  other arithmetic  3.31 us (2%)
    pallas_call x1, Pallas kernels, second_products(): pl.pallas_call(functools.partial(second_kernel, chunk, batch), grid_spec=...  46.8 us
    pmax x2, blocking collectives, final_exchange(): return (own, lax.pmax(f_new, ('row', 'dp')), lax.pmax(u_new, ('col', 'dp')))  42 us
    psum x1, waiting for transfers between devices, hidden_exchange(): total = lax.psum(mine, 'col').astype(jnp.float32)  28 us
    all_gather x1, blocking collectives, gather_inputs(): return lax.all_gather(own, ('dp', 'row'), axis=0, tiled=False)  27.6 us
    pallas_call x1, Pallas kernels, first_products(): pl.pallas_call(functools.partial(first_kernel, chunk, batch), grid_spec=p...  17.8 us
    reduce_scatter x1, waiting for transfers between devices, hidden_exchange(): mine = lax.psum_scatter(partial, 'dp', scatter_dimension=0, tiled=False)  9.61 us
  transfers between devices with their start and end apart: 3, of which 2 were waited for; matrix products, arithmetic and copies ran while one was open for 1% of the time, Pallas kernels for 0%

profile of v1, /device:TPU:0, one launch (start us, length us, event | category | flops | bytes accessed | tf_op | source)
XLA Modules:
  0.0 201.0 jit_solution(140204861800544656)
XLA Ops:
  7.2 0.0 reduce-scatter.3.cloned.1.call-start
  7.2 0.8 pad_maximum_fusion.1
  8.0 0.8 copy.23
  8.9 0.8 reshape.70.up_at
  9.7 0.8 copy.24
  10.5 0.8 reshape.71.down_at
  11.4 27.6 %all_gather.6 = bf16[8,192,128]{2,1,0:T(8,128)(2,1)S(1)} all-gather(bf16[1,192,128]{2,1,0:T(8,128)(2,1)S(1)} %all_gather_reshape.3), channel_id=1, replica_groups=mesh['groups'=2,'row'=4,'col'=2,'dp'=2] {'dp','row'}, dimensions={0}, use_global_device_ids=true | all-gather | bytes 442368 | tf_op jit(solution)/shard_map/all_gather | solution.py:297
  38.9 0.2 copy.25
  39.1 0.8 pad.4.x_ref
  39.9 0.0 copy-start.2
  39.9 0.0 copy-start.3
  39.9 0.0 copy-start
  39.9 0.0 copy-start.1
  39.9 17.8 %shard_map.170 = bf16[2,2,48,16,128]{4,3,2,1,0:T(8,128)(2,1)} custom-call(s32[1152]{0:T(1024)} %reshape.70.up_at, s32[1152]{0:T(1024)} %reshape.71.down_at, s32[2]{0:T(128)} %bitcast.46, s32[1]{0:T(128)} %bitcast.1.place, bf16[2,25,32,128]{3,2,1,0:T(8,128)(2,1)} %pad.4.x_ref, bf16[576,128,128]{2,1,0:T(8,128)(2,1)} %bitcast.31, bf16[576,128,128]{2,1,0:T(8,128)(2,1)} %bitcast.33), custom_call_target="tpu_custom_call" | custom-call | flops 603979776 | bytes 18874368 | tf_op jit(solution)/shard_map/pallas_call | solution.py:76
  57.7 0.0 reduce-scatter.3.cloned.1.call-update
  57.7 0.0 all-reduce.3.cloned.1.call-start
  57.7 9.6 %reduce-scatter.3.cloned.1.call-done = bf16[1,2,48,16,128]{4,3,2,1,0:T(8,128)(2,1)} async-done(((bf16[2,2,48,16,128]{4,3,2,1,0:T(8,128)(2,1)}), bf16[1,2,48,16,128]{4,3,2,1,0:T(8,128)(2,1)}) %reduce-scatter.3.cloned.1.call-update) | async-done | bytes 393232 | tf_op jit(solution)/shard_map/reduce_scatter | solution.py:306
  67.3 0.0 all-reduce.3.cloned.1.call-update
  67.4 0.0 reduce-scatter.5.cloned.1.call-start
  67.4 0.0 copy-done.2
  67.4 0.0 copy-done.3
  67.4 0.6 pad_maximum_fusion.3.f_cover
  68.0 0.0 copy-done
  68.0 0.0 copy-done.1
  68.0 0.6 pad_maximum_fusion.2.u_cover
  68.7 28.0 %all-reduce.3.cloned.1.call-done = bf16[2,48,16,128]{3,2,1,0:T(8,128)(2,1)} async-done(((bf16[2,48,16,128]{3,2,1,0:T(8,128)(2,1)}), bf16[2,48,16,128]{3,2,1,0:T(8,128)(2,1)}) %all-reduce.3.cloned.1.call-update) | async-done | bytes 393232 | tf_op jit(solution)/shard_map/psum | solution.py:307
  96.6 1.0 convert_element_type.6
  97.7 0.2 multiply_convert_fusion
  97.9 2.5 %all_gather.7.h_ref = bf16[2,48,32,128]{3,2,1,0:T(8,128)(2,1)} all-gather(bf16[2,48,16,128]{3,2,1,0:T(8,128)(2,1)S(1)} %pad_maximum_fusion), channel_id=1, replica_groups=mesh['groups'=2,'row'=4,'col'=2,'dp'=2] {'dp'}, dimensions={2}, use_global_device_ids=true | all-gather | bytes 1179648 | tf_op jit(solution)/shard_map/all_gather | solution.py:310
  100.4 46.8 %shard_map.171 = (bf16[1,1,288,128,128]{4,3,2,1,0:T(8,128)(2,1)}, bf16[1,1,288,128,128]{4,3,2,1,0:T(8,128)(2,1)}, bf16[2,24,32,128]{3,2,1,0:T(8,128)(2,1)}, f32[2,24,128]{2,1,0:T(8,128)}, f32[2,48,128]{2,1,0:T(8,128)}) custom-call(s32[1152]{0:T(1024)} %reshape.70.up_at, s32[1152]{0:T(1024)} %reshape.71.down_at, s32[2]{0:T(128)} %bitcast.47, s32[1]{0:T(128)} %bitcast.1.place, ...), custom_call_target="tpu_custom_call" | custom-call | flops 1207959552 | bytes 37748736 | tf_op jit(solution)/shard_map/pallas_call | solution.py:249
  147.2 1.9 copy.26
  149.2 0.0 reduce-scatter.5.cloned.1.call-update
  149.2 30.9 %pmax.14 = f32[2,24,128]{2,1,0:T(8,128)S(1)} all-reduce(f32[2,24,128]{2,1,0:T(8,128)} %get-tuple-element.16), channel_id=1, replica_groups=mesh['groups'=2,'row'=4,'col'=2,'dp'=2] {'row','dp'}, use_global_device_ids=true, to_apply=%region_3.4 | all-reduce | flops 6144 | bytes 49152 | tf_op jit(solution)/shard_map/pmax | solution.py:315
  180.1 11.1 %pmax.15 = f32[2,48,128]{2,1,0:T(8,128)S(1)} all-reduce(f32[2,48,128]{2,1,0:T(8,128)} %get-tuple-element.17), channel_id=1, replica_groups=mesh['groups'=2,'row'=4,'col'=2,'dp'=2] {'col','dp'}, use_global_device_ids=true, to_apply=%region_4.5 | all-reduce | flops 12288 | bytes 98304 | tf_op jit(solution)/shard_map/pmax | solution.py:315
  191.2 0.6 slice_bitcast_fusion.2
  191.8 0.6 slice_bitcast_fusion
  192.4 0.0 reduce-scatter.5.cloned.1.call-done
  192.5 0.8 fusion.1
  193.2 0.6 squeeze.21
  193.8 0.6 squeeze.20
  (2 shorter events, 0.1 us)
Async XLA Ops:
  7.2 60.2 %reduce-scatter.3.cloned.1.call-start = ((), (), s32[]{:S(2)}) async-start(), calls=%async_computation.2 | async-start | bytes 1179648 | tf_op jit(solution)/shard_map/reduce_scatter | solution.py:306
  39.9 27.5 %copy-start.2 = (f32[3072]{0:T(1024)S(1)}, f32[3072]{0:T(1024)}, u32[]{:S(2)}) copy-start(f32[3072]{0:T(1024)} %param.21) | copy-start | bytes 36868
  39.9 27.5 %copy-start.3 = (f32[3072]{0:T(1024)S(1)}, f32[3072]{0:T(1024)}, u32[]{:S(2)}) copy-start(f32[3072]{0:T(1024)} %param.18) | copy-start | bytes 36868
  39.9 28.1 %copy-start = (f32[6144]{0:T(1024)S(1)}, f32[6144]{0:T(1024)}, u32[]{:S(2)}) copy-start(f32[6144]{0:T(1024)} %param.20) | copy-start | bytes 73732
  39.9 28.1 %copy-start.1 = (f32[6144]{0:T(1024)S(1)}, f32[6144]{0:T(1024)}, u32[]{:S(2)}) copy-start(f32[6144]{0:T(1024)} %param.19) | copy-start | bytes 73732
  57.7 38.9 %all-reduce.3.cloned.1.call-start = ((), (), s32[]{:S(2)}) async-start(), calls=%async_computation.3 | async-start | bytes 786432 | tf_op jit(solution)/shard_map/psum | solution.py:307
  67.4 125.1 %reduce-scatter.5.cloned.1.call-start = ((), (), s32[]{:S(2)}) async-start(), calls=%async_computation.4 | async-start | bytes 442368 | tf_op jit(solution)/shard_map/reduce_scatter | solution.py:314
Sparse Core Ops, SparseCore 0:
  57.8 9.4 reduce-scatter.2
  69.7 26.8 all-reduce.2
  149.3 31.9 reduce-scatter.4

commit v2 on v1

--- a/solution.py
+++ b/solution.py
@@ -138,7 +138,7 @@
 ):
     step = pl.program_id(0)
     features = x_ref.shape[1] - 1
-    units = h_ref.shape[1]
+    shares, _, units, share_rows, _ = h_ref.shape
     width = x_ref.shape[-1]
     groups = width // 8
 
@@ -167,9 +167,11 @@
 
         @pl.loop(0, units)
         def _(u):
-            act[u] = h_ref[0, u]
-            dh[u] = h_ref[1, u]
-            act_turned[u] = h_ref[0, u].astype(jnp.float32).T.astype(jnp.bfloat16)
+            for share in range(shares):
+                at = pl.ds(share * share_rows, share_rows)
+                act[u, at] = h_ref[share, 0, u]
+                dh[u, at] = h_ref[share, 1, u]
+            act_turned[u] = act[u].astype(jnp.float32).T.astype(jnp.bfloat16)
             wide = jnp.broadcast_to(u_cover[1, pl.ds(u, 1)], (width, width)).T
             u_rows[u] = wide
             u_rows_max[u] = wide
@@ -230,7 +232,7 @@
     slots = up_weight.shape[0] // shares
     _, features1, tokens, width = x.shape
     features = features1 - 1
-    units = h.shape[1]
+    units = h.shape[2]
     chunk = largest_divisor(slots, 24)
     batch = largest_divisor(chunk, 4)
     steps = slots // chunk
@@ -293,26 +295,292 @@
     )(up_at, down_at, counts, place, x, h, up_weight, down_weight, f_cover, u_cover)
 
 
-def gather_inputs(own):
-    return lax.all_gather(own, ("dp", "row"), axis=0, tiled=False)
-
-
 def silu_pair(hidden):
     sigma = 1.0 / (1.0 + jnp.exp(-hidden))
     return hidden * sigma, sigma * (1.0 + hidden * (1.0 - sigma))
 
 
+def others(axis):
+    size, me = lax.axis_size(axis), lax.axis_index(axis)
+    return [{axis: lax.rem(me + k, size)} for k in range(1, size)]
+
+
+def meet(devices):
+    barrier = pltpu.get_barrier_semaphore()
+    for device in devices:
+        pl.semaphore_signal(barrier, inc=1, device_id=device, device_id_type=MESH)
+    pl.semaphore_wait(barrier, len(devices))
+
+
+def send(source, target, send_sem, recv_sem, device):
+    copy = pltpu.make_async_remote_copy(
+        src_ref=source,
+        dst_ref=target,
+        send_sem=send_sem,
+        recv_sem=recv_sem,
+        device_id=device,
+        device_id_type=MESH,
+    )
+    copy.start()
+    return copy
+
+
+def comm_call(kernel, name, collective_id, out_shape, scratch_shapes, args):
+    outs = jax.tree.map(lambda _: pl.BlockSpec(memory_space=pltpu.VMEM), out_shape)
+    return pl.pallas_call(
+        kernel,
+        name=name,
+        out_shape=out_shape,
+        in_specs=[pl.BlockSpec(memory_space=pltpu.VMEM)] * len(args),
+        out_specs=outs,
+        scratch_shapes=scratch_shapes,
+        compiler_params=pltpu.CompilerParams(
+            collective_id=collective_id, has_side_effects=True, vmem_limit_bytes=VMEM_LIMIT
+        ),
+    )(*args)
+
+
+def gather_kernel(own_ref, out_ref, row_send, row_recv, dp_send, dp_recv):
+    size, me, share = lax.axis_size("row"), lax.axis_index("row"), lax.axis_index("dp")
+    peers, partner = others("row"), others("dp")[0]
+    meet(peers + [partner])
+    mine = out_ref.at[share * size + me]
+    row_copies = [
+        send(own_ref, mine, row_send.at[k], row_recv.at[k], peer) for k, peer in enumerate(peers)
+    ]
+    dp_copies = [send(own_ref, mine, dp_send.at[size - 1], dp_recv.at[size - 1], partner)]
+    out_ref[share * size + me] = own_ref[...]
+    for k, copy in enumerate(row_copies):
+        copy.wait_recv()
+        landed = out_ref.at[share * size + lax.rem(me + size - k - 1, size)]
+        dp_copies.append(send(landed, landed, dp_send.at[k], dp_recv.at[k], partner))
+    for copy in dp_copies:
+        copy.wait_recv()
+    for copy in row_copies + dp_copies:
+        copy.wait_send()
+
+
+def gather_inputs(own):
+    size = lax.axis_size("row")
+    dma = pltpu.SemaphoreType.DMA
+    return comm_call(
+        gather_kernel,
+        "gather_inputs",
+        0,
+        jax.ShapeDtypeStruct((2 * size,) + own.shape, own.dtype),
+        [dma((size,)), dma((size,)), dma((size,)), dma((size,))],
+        (own,),
+    )
+
+
+def hidden_kernel(
+    pieces,
+    part_ref,
+    h_ref,
+    from_dp,
+    mine,
+    from_col,
+    dp_send,
+    dp_recv,
+    col_send,
+    col_recv,
+    last_send,
+    last_recv,
+):
+    share = lax.axis_index("dp")
+    peers, partner = others("col"), others("dp")[0]
+    depth = part_ref.shape[2] // pieces
+    meet(peers + [partner])
+    cuts = [pl.ds(c * depth, depth) for c in range(pieces)]
+    dp_copies = [
+        send(
+            part_ref.at[1 - share, :, cut],
+            from_dp.at[:, cut],
+            dp_send.at[c],
+            dp_recv.at[c],
+            partner,
+        )
+        for c, cut in enumerate(cuts)
+    ]
+    col_copies = []
+    for c, cut in enumerate(cuts):
+        dp_copies[c].wait_recv()
+        total = part_ref[share, :, cut].astype(jnp.float32) + from_dp[:, cut].astype(jnp.float32)
+        mine[:, cut] = total.astype(jnp.bfloat16)
+        col_copies.append(
+            [
+                send(
+                    mine.at[:, cut],
+                    from_col.at[k, :, cut],
+                    col_send.at[c, k],
+                    col_recv.at[c, k],
+                    peer,
+                )
+                for k, peer in enumerate(peers)
+            ]
+        )
+    last_copies = []
+    for c, cut in enumerate(cuts):
+        total = mine[:, cut].astype(jnp.float32)
+        for k, copy in enumerate(col_copies[c]):
+            copy.wait_recv()
+            total = total + from_col[k, :, cut].astype(jnp.float32)
+        activation, slope = silu_pair(total[0])
+        h_ref[share, 0, cut] = activation.astype(jnp.bfloat16)
+        h_ref[share, 1, cut] = (total[1] * slope).astype(jnp.bfloat16)
+        done = h_ref.at[share, :, cut]
+        last_copies.append(send(done, done, last_send.at[c], last_recv.at[c], partner))
+    for copy in last_copies:
+        copy.wait_recv()
+    for copy in dp_copies + sum(col_copies, []) + last_copies:
+        copy.wait_send()
+
+
 def hidden_exchange(partial):
-    mine = lax.psum_scatter(partial, "dp", scatter_dimension=0, tiled=False)
-    total = lax.psum(mine, "col").astype(jnp.float32)
-    activation, slope = silu_pair(total[0])
-    both = jnp.stack([activation, total[1] * slope]).astype(jnp.bfloat16)
-    return lax.all_gather(both, "dp", axis=2, tiled=True)
+    pieces = largest_divisor(partial.shape[2], 6)
+    peers = lax.axis_size("col") - 1
+    dma = pltpu.SemaphoreType.DMA
+    piece = partial.shape[1:]
+    return comm_call(
+        functools.partial(hidden_kernel, pieces),
+        "hidden_exchange",
+        1,
+        jax.ShapeDtypeStruct(partial.shape, jnp.bfloat16),
+        [
+            pltpu.VMEM(piece, jnp.bfloat16),
+            pltpu.VMEM(piece, jnp.bfloat16),
+            pltpu.VMEM((peers,) + piece, jnp.bfloat16),
+            dma((pieces,)),
+            dma((pieces,)),
+            dma((pieces, peers)),
+            dma((pieces, peers)),
+            dma((pieces,)),
+            dma((pieces,)),
+        ],
+        (partial,),
+    )
+
+
+def final_kernel(
+    sums_ref,
+    f_ref,
+    u_ref,
+    out_ref,
+    f_out,
+    u_out,
+    from_dp,
+    to_row,
+    from_row,
+    f_dp,
+    u_dp,
+    f_row,
+    u_col,
+    dp_send,
+    dp_recv,
+    row_send,
+    row_recv,
+    max_send,
+    max_recv,
+    f_send,
+    f_recv,
+    u_send,
+    u_recv,
+):
+    size, me, share = lax.axis_size("row"), lax.axis_index("row"), lax.axis_index("dp")
+    peers, columns, partner = others("row"), others("col"), others("dp")[0]
+    meet(peers + columns + [partner])
+    targets = [lax.rem(me + k, size) for k in range(1, size)] + [me]
+    dp_copies = [
+        send(
+            sums_ref.at[(1 - share) * size + target],
+            from_dp.at[k],
+            dp_send.at[k],
+            dp_recv.at[k],
+            partner,
+        )
+        for k, target in enumerate(targets)
+    ]
+    max_copies = [
+        send(f_ref, f_dp, max_send.at[0], max_recv.at[0], partner),
+        send(u_ref, u_dp, max_send.at[1], max_recv.at[1], partner),
+    ]
+    row_copies = []
+    for k, target in enumerate(targets):
+        dp_copies[k].wait_recv()
+        total = sums_ref[share * size + target].astype(jnp.float32)
+        total = total + from_dp[k].astype(jnp.float32)
+        if k < size - 1:
+            to_row[k] = total.astype(jnp.bfloat16)
+            row_copies.append(
+                send(to_row.at[k], from_row.at[k], row_send.at[k], row_recv.at[k], peers[k])
+            )
+    max_copies[0].wait_recv()
+    max_copies[0].wait_send()
+    f_out[...] = jnp.maximum(f_ref[...], f_dp[...])
+    max_copies[1].wait_recv()
+    max_copies[1].wait_send()
+    u_out[...] = jnp.maximum(u_ref[...], u_dp[...])
+    f_own = f_out[...]
+    f_dp[...] = f_own
+    u_own = u_out[...]
+    u_dp[...] = u_own
+    f_copies = [
+        send(f_dp, f_row.at[k], f_send.at[k], f_recv.at[k], peer) for k, peer in enumerate(peers)
+    ]
+    u_copies = [
+        send(u_dp, u_col.at[k], u_send.at[k], u_recv.at[k], peer) for k, peer in enumerate(columns)
+    ]
+    for k, copy in enumerate(u_copies):
+        copy.wait_recv()
+        u_own = jnp.maximum(u_own, u_col[k])
+    u_out[...] = u_own
+    for k, copy in enumerate(row_copies):
+        copy.wait_recv()
+        total = total + from_row[k].astype(jnp.float32)
+    out_ref[...] = total.astype(jnp.bfloat16)
+    for k, copy in enumerate(f_copies):
+        copy.wait_recv()
+        f_own = jnp.maximum(f_own, f_row[k])
+    f_out[...] = f_own
+    for copy in dp_copies + row_copies + f_copies + u_copies:
+        copy.wait_send()
 
 
 def final_exchange(sums, f_new, u_new):
-    own = lax.psum_scatter(sums, ("dp", "row"), scatter_dimension=0, tiled=False)
-    return own, lax.pmax(f_new, ("row", "dp")), lax.pmax(u_new, ("col", "dp"))
+    size, columns = lax.axis_size("row"), lax.axis_size("col")
+    dma = pltpu.SemaphoreType.DMA
+    f32, bf16 = jnp.float32, jnp.bfloat16
+    piece = sums.shape[1:]
+    return comm_call(
+        final_kernel,
+        "final_exchange",
+        2,
+        (
+            jax.ShapeDtypeStruct(piece, bf16),
+            jax.ShapeDtypeStruct(f_new.shape, f32),
+            jax.ShapeDtypeStruct(u_new.shape, f32),
+        ),
+        [
+            pltpu.VMEM((size,) + piece, bf16),
+            pltpu.VMEM((size - 1,) + piece, bf16),
+            pltpu.VMEM((size - 1,) + piece, bf16),
+            pltpu.VMEM(f_new.shape, f32),
+            pltpu.VMEM(u_new.shape, f32),
+            pltpu.VMEM((size - 1,) + f_new.shape, f32),
+            pltpu.VMEM((columns - 1,) + u_new.shape, f32),
+            dma((size,)),
+            dma((size,)),
+            dma((size - 1,)),
+            dma((size - 1,)),
+            dma((2,)),
+            dma((2,)),
+            dma((size - 1,)),
+            dma((size - 1,)),
+            dma((columns - 1,)),
+            dma((columns - 1,)),
+        ],
+        (sums, f_new, u_new),
+    )
 
 
 def on_device(

time: 202 us -> 124 us (0.61)
  blocking collectives: 72.1 us -> 0 us
  Pallas kernels: 64.6 us -> 107 us
  waiting for transfers between devices: 37.6 us -> 0 us
  between operations: 13.8 us -> 0.69 us
  local copies, waits for them, and re-layouts: 9.4 us -> 12.5 us
    pmax x2 -> x0, blocking collectives: 42 us -> none  [final_exchange(): return (own, lax.pmax(f_new, ('row', 'dp')), lax.pmax(u_new, ('col', 'dp')))]
    pallas_call x0 -> x3, Pallas kernels: none -> 41.9 us  [comm_call(): pl.pallas_call(kernel, name=name, out_shape=out_shape, in_specs=[pl.Block...]
    all_gather x2 -> x0, blocking collectives: 30.1 us -> none  [the longest x1 27.6 us: gather_inputs(): return lax.all_gather(own, ('dp', 'row'), axis=0, tiled=False)]
    psum x1 -> x0, waiting for transfers between devices: 28 us -> none  [hidden_exchange(): total = lax.psum(mine, 'col').astype(jnp.float32)]
    reduce_scatter x2 -> x0, waiting for transfers between devices: 9.61 us -> none  [the longest x1 9.61 us: hidden_exchange(): mine = lax.psum_scatter(partial, 'dp', scatter_dimension=0, tiled=False)]
  transfers between devices with their start and end apart: 3 -> 0, of which waited for: 2 -> 0; matrix products, arithmetic and copies ran while one was open for 1% -> 0% of each run, Pallas kernels for 0% -> 0%
where the time goes in v2:
time: 124 us; the launch traced here: 123 us
  Pallas kernels  107 us (86%)
  local copies, waits for them, and re-layouts  12.5 us (10%)
  other arithmetic  3.5 us (3%)
    pallas_call x1, Pallas kernels, second_products(): pl.pallas_call(functools.partial(second_kernel, chunk, batch), grid_spec=...  47 us
    pallas_call x3, Pallas kernels, comm_call(): pl.pallas_call(kernel, name=name, out_shape=out_shape, in_specs=[pl.Block...  41.9 us
    pallas_call x1, Pallas kernels, first_products(): pl.pallas_call(functools.partial(first_kernel, chunk, batch), grid_spec=p...  17.6 us

profile of v2, /device:TPU:0, one launch (start us, length us, event | category | flops | bytes accessed | tf_op | source)
XLA Modules:
  0.0 123.2 jit_solution(14610280628186195702)
XLA Ops:
  0.6 1.3 %pad_maximum_fusion.2.f_cover = f32[2,24,128]{2,1,0:T(8,128)} fusion(f32[1,24,128]{2,1,0:T(8,128)} %bitcast.42, f32[1,24,128]{2,1,0:T(8,128)} %bitcast.43), kind=kLoop, calls=%fused_computation.2 | loop fusion | flops 6144 | bytes 49152 | tf_op jit(solution)/shard_map/stack | solution.py:624
  2.0 0.8 pad_maximum_fusion
  2.8 0.6 reshape.78.own_ref
  3.4 1.4 %pad_maximum_fusion.1.u_cover = f32[2,48,128]{2,1,0:T(8,128)} fusion(f32[1,48,128]{2,1,0:T(8,128)} %bitcast.40, f32[1,48,128]{2,1,0:T(8,128)} %bitcast.41), kind=kLoop, calls=%fused_computation.1 | loop fusion | flops 12288 | bytes 98304 | tf_op jit(solution)/shard_map/stack | solution.py:625
  4.8 0.8 copy.21
  5.6 0.8 reshape.74.up_at
  6.4 0.8 copy.22
  7.3 0.8 reshape.75.down_at
  8.1 12.3 %gather_inputs.1 = bf16[8,192,128]{2,1,0:T(8,128)(2,1)} custom-call(bf16[192,128]{1,0:T(8,128)(2,1)} %reshape.78.own_ref), custom_call_target="tpu_custom_call" | custom-call | tf_op jit(solution)/shard_map/gather_inputs/pallas_call | solution.py:330
  20.4 1.1 copy.23
  21.6 0.8 pad.4.x_ref
  22.3 17.6 %shard_map.170.part_ref = bf16[2,2,48,16,128]{4,3,2,1,0:T(8,128)(2,1)} custom-call(s32[1152]{0:T(1024)} %reshape.74.up_at, s32[1152]{0:T(1024)} %reshape.75.down_at, s32[2]{0:T(128)} %bitcast.44, s32[1]{0:T(128)} %bitcast.1.place, bf16[2,25,32,128]{3,2,1,0:T(8,128)(2,1)} %pad.4.x_ref, bf16[576,128,128]{2,1,0:T(8,128)(2,1)} %bitcast.30, ...), custom_call_target="tpu_custom_call" | custom-call | flops 603979776 | bytes 18874368 | tf_op jit(solution)/shard_map/pallas_call | solution.py:76
  40.0 15.9 %hidden_exchange.1.h_ref = bf16[2,2,48,16,128]{4,3,2,1,0:T(8,128)(2,1)} custom-call(bf16[2,2,48,16,128]{4,3,2,1,0:T(8,128)(2,1)} %shard_map.170.part_ref), custom_call_target="tpu_custom_call" | custom-call | tf_op jit(solution)/shard_map/hidden_exchange/pallas_call | solution.py:330
  55.8 47.0 %shard_map.171 = (bf16[1,1,288,128,128]{4,3,2,1,0:T(8,128)(2,1)}, bf16[1,1,288,128,128]{4,3,2,1,0:T(8,128)(2,1)}, bf16[2,24,32,128]{3,2,1,0:T(8,128)(2,1)}, f32[2,24,128]{2,1,0:T(8,128)}, f32[2,48,128]{2,1,0:T(8,128)}) custom-call(s32[1152]{0:T(1024)} %reshape.74.up_at, s32[1152]{0:T(1024)} %reshape.75.down_at, s32[2]{0:T(128)} %bitcast.45, s32[1]{0:T(128)} %bitcast.1.place, ...), custom_call_target="tpu_custom_call" | custom-call | flops 1207959552 | bytes 37748736 | tf_op jit(solution)/shard_map/pallas_call | solution.py:251
  102.9 1.9 %copy.24 = bf16[2,24,8,4,128]{4,1,3,0,2:T(8,128)(2,1)} copy(bf16[2,24,8,4,128]{4,3,2,1,0:T(4,128)(2,1)} %bitcast.37) | data formatting | bytes 786432 | tf_op jit(solution)/shard_map/reshape | solution.py:629
  104.8 13.7 %final_exchange.1 = (bf16[192,128]{1,0:T(8,128)(2,1)}, f32[2,24,128]{2,1,0:T(8,128)}, f32[2,48,128]{2,1,0:T(8,128)}) custom-call(bf16[8,192,128]{2,1,0:T(8,128)(2,1)} %bitcast.34, f32[2,24,128]{2,1,0:T(8,128)} %get-tuple-element.17.f_ref, f32[2,48,128]{2,1,0:T(8,128)} %get-tuple-element.18.u_ref), custom_call_target="tpu_custom_call" | custom-call | tf_op jit(solution)/shard_map/final_exchange/pallas_call | solution.py:330
  118.5 0.8 fusion
  119.3 0.6 squeeze.19
  119.9 0.6 squeeze.18
  120.5 1.3 %slice_bitcast_fusion.2 = (f32[3072]{0:T(1024)}, f32[3072]{0:T(1024)}) fusion(f32[2,24,128]{2,1,0:T(8,128)} %get-tuple-element.22), kind=kLoop, calls=%fused_computation.5 | loop fusion | bytes 49152 | tf_op jit(solution)/shard_map/squeeze | solution.py:635
  121.9 1.4 %slice_bitcast_fusion = (f32[6144]{0:T(1024)}, f32[6144]{0:T(1024)}) fusion(f32[2,48,128]{2,1,0:T(8,128)} %get-tuple-element.23), kind=kLoop, calls=%fused_computation.3 | loop fusion | bytes 98304 | tf_op jit(solution)/shard_map/squeeze | solution.py:635

commit v3 on v2

--- a/solution.py
+++ b/solution.py
@@ -23,16 +23,17 @@
 
 def slot_places(index_ref, slot, live, features, units):
     alive = slot < live
-    feature = jnp.where(alive, index_ref[2 * slot], features)
+    read = index_ref[2 * slot]
+    feature = jnp.where(alive, read, features)
     unit = jnp.where(alive, index_ref[2 * slot + 1], units)
-    return feature, unit
+    return read, feature, unit
 
 
 def first_kernel(
     chunk, batch, up_at, down_at, counts, place, x_ref, up_ref, down_ref, out_ref, hid, dac
 ):
     step = pl.program_id(0)
-    features = x_ref.shape[1] - 1
+    features = x_ref.shape[1]
     units = hid.shape[0] - 1
     shares, _, _, share_rows, _ = out_ref.shape
 
@@ -49,10 +50,10 @@
         for j in range(batch):
             at = part * batch + j
             slot = first + at
-            uf, uu = slot_places(up_at, slot, counts[0], features, units)
-            df, du = slot_places(down_at, slot, counts[1], features, units)
-            work.append((uu, dot(x_ref[0, uf], up_ref[at], NN), hid))
-            work.append((du, dot(x_ref[1, df], down_ref[at], NT), dac))
+            ux, uf, uu = slot_places(up_at, slot, counts[0], features, units)
+            dx, df, du = slot_places(down_at, slot, counts[1], features, units)
+            work.append((uu, dot(x_ref[0, ux], up_ref[at], NN), hid))
+            work.append((du, dot(x_ref[1, dx], down_ref[at], NT), dac))
         for unit, product, total in work:
             total[unit] += product
 
@@ -66,9 +67,9 @@
 
 def first_products(up_at, down_at, counts, place, x, up_weight, down_weight, units, shares):
     slots = up_weight.shape[0] // shares
-    _, features1, tokens, width = x.shape
-    chunk = largest_divisor(slots, 24)
-    batch = largest_divisor(chunk, 8)
+    _, _, tokens, width = x.shape
+    chunk = largest_divisor(slots, 48)
+    batch = chunk
     steps = slots // chunk
     weight = pl.BlockSpec(
         (chunk, width, width), lambda i, a, b, c, p: (p[0] * steps + i, 0, 0)
@@ -114,13 +115,17 @@
     h_ref,
     up_ref,
     down_ref,
-    f_cover,
-    u_cover,
+    up_rows,
+    up_cols,
+    down_rows,
+    down_cols,
     up_step,
     down_step,
     sums_ref,
-    f_new,
-    u_new,
+    up_rows_new,
+    up_cols_new,
+    down_rows_new,
+    down_cols_new,
     x_turned,
     act_turned,
     dh,
@@ -137,7 +142,7 @@
     tok,
 ):
     step = pl.program_id(0)
-    features = x_ref.shape[1] - 1
+    features = x_ref.shape[1]
     shares, _, units, share_rows, _ = h_ref.shape
     width = x_ref.shape[-1]
     groups = width // 8
@@ -157,25 +162,25 @@
         f_cols_max[...] = jnp.zeros_like(f_cols_max)
         u_cols_max[...] = jnp.zeros_like(u_cols_max)
 
-        @pl.loop(0, features)
+        @pl.loop(0, features, unroll=largest_divisor(features, 8))
         def _(f):
             x_turned[f] = x_ref[0, f].astype(jnp.float32).T.astype(jnp.bfloat16)
-            wide = jnp.broadcast_to(f_cover[0, pl.ds(f, 1)], (width, width)).T
+            wide = jnp.broadcast_to(up_rows[pl.ds(f, 1)], (width, width)).T
             f_rows[f] = wide
             f_rows_max[f] = wide
-            f_cols[f] = f_cover[1, pl.ds(f, 1)]
-
-        @pl.loop(0, units)
+            f_cols[f] = down_cols[pl.ds(f, 1)]
+
+        @pl.loop(0, units, unroll=largest_divisor(units, 8))
         def _(u):
             for share in range(shares):
                 at = pl.ds(share * share_rows, share_rows)
                 act[u, at] = h_ref[share, 0, u]
                 dh[u, at] = h_ref[share, 1, u]
             act_turned[u] = act[u].astype(jnp.float32).T.astype(jnp.bfloat16)
-            wide = jnp.broadcast_to(u_cover[1, pl.ds(u, 1)], (width, width)).T
+            wide = jnp.broadcast_to(down_rows[pl.ds(u, 1)], (width, width)).T
             u_rows[u] = wide
             u_rows_max[u] = wide
-            u_cols[u] = u_cover[0, pl.ds(u, 1)]
+            u_cols[u] = up_cols[pl.ds(u, 1)]
 
     first = place[0] * (chunk * pl.num_programs(0)) + step * chunk
 
@@ -192,8 +197,8 @@
         for j in range(batch):
             at = part * batch + j
             slot = first + at
-            uf, uu = slot_places(up_at, slot, counts[0], features, units)
-            df, du = slot_places(down_at, slot, counts[1], features, units)
+            ux, uf, uu = slot_places(up_at, slot, counts[0], features, units)
+            dx, df, du = slot_places(down_at, slot, counts[1], features, units)
             work.append((uf, dot(dh[uu], up_ref[at], NT), tok))
             work.append((df, dot(act[du], down_ref[at], NN), mix))
         for feature, product, total in work:
@@ -201,10 +206,10 @@
         for j in range(batch):
             at = part * batch + j
             slot = first + at
-            uf, uu = slot_places(up_at, slot, counts[0], features, units)
-            df, du = slot_places(down_at, slot, counts[1], features, units)
+            ux, uf, uu = slot_places(up_at, slot, counts[0], features, units)
+            dx, df, du = slot_places(down_at, slot, counts[1], features, units)
             up_grad = dot(x_turned[uf], dh[uu], NN)
-            down_grad = dot(act_turned[du], x_ref[1, df], NN)
+            down_grad = dot(act_turned[du], x_ref[1, dx], NN)
             one_step(up_grad, f_rows, u_cols, f_rows_max, u_cols_max, uf, uu, up_step, at)
             one_step(down_grad, u_rows, f_cols, u_rows_max, f_cols_max, du, df, down_step, at)
 
@@ -213,28 +218,27 @@
         sums_ref[0] = mix[:features].astype(jnp.bfloat16)
         sums_ref[1] = tok[:features].astype(jnp.bfloat16)
 
-        @pl.loop(0, features)
+        @pl.loop(0, features, unroll=largest_divisor(features, 8))
         def _(f):
-            f_new[0, pl.ds(f, 1)] = jnp.max(f_rows_max[f].T, axis=0, keepdims=True)
+            up_rows_new[pl.ds(f, 1)] = jnp.max(f_rows_max[f].T, axis=0, keepdims=True)
             best = jnp.max(f_cols_max[f], axis=0, keepdims=True)
-            f_new[1, pl.ds(f, 1)] = jnp.maximum(best, f_cols[f])
-
-        @pl.loop(0, units)
+            down_cols_new[pl.ds(f, 1)] = jnp.maximum(best, f_cols[f])
+
+        @pl.loop(0, units, unroll=largest_divisor(units, 8))
         def _(u):
-            u_new[1, pl.ds(u, 1)] = jnp.max(u_rows_max[u].T, axis=0, keepdims=True)
+            down_rows_new[pl.ds(u, 1)] = jnp.max(u_rows_max[u].T, axis=0, keepdims=True)
             best = jnp.max(u_cols_max[u], axis=0, keepdims=True)
-            u_new[0, pl.ds(u, 1)] = jnp.maximum(best, u_cols[u])
+            up_cols_new[pl.ds(u, 1)] = jnp.maximum(best, u_cols[u])
 
 
 def second_products(
-    up_at, down_at, counts, place, x, h, up_weight, down_weight, f_cover, u_cover, shares
+    up_at, down_at, counts, place, x, h, up_weight, down_weight, covers, shares
 ):
     slots = up_weight.shape[0] // shares
-    _, features1, tokens, width = x.shape
-    features = features1 - 1
+    _, features, tokens, width = x.shape
     units = h.shape[2]
     chunk = largest_divisor(slots, 24)
-    batch = largest_divisor(chunk, 4)
+    batch = chunk
     steps = slots // chunk
     weight = pl.BlockSpec(
         (chunk, width, width), lambda i, a, b, c, p: (p[0] * steps + i, 0, 0)
@@ -258,10 +262,14 @@
                 whole(h.shape),
                 weight,
                 weight,
-                whole(f_cover.shape),
-                whole(u_cover.shape),
+                *[whole(cover.shape) for cover in covers],
             ],
-            out_specs=[stepped, stepped, whole(sums), whole(f_cover.shape), whole(u_cover.shape)],
+            out_specs=[
+                stepped,
+                stepped,
+                whole(sums),
+                *[whole(cover.shape) for cover in covers],
+            ],
             scratch_shapes=[
                 pltpu.VMEM((features + 1, width, tokens), bf16),
                 pltpu.VMEM((units + 1, width, tokens), bf16),
@@ -283,8 +291,7 @@
             jax.ShapeDtypeStruct((1, 1, slots, width, width), bf16),
             jax.ShapeDtypeStruct((1, 1, slots, width, width), bf16),
             jax.ShapeDtypeStruct(sums, bf16),
-            jax.ShapeDtypeStruct(f_cover.shape, f32),
-            jax.ShapeDtypeStruct(u_cover.shape, f32),
+            *[jax.ShapeDtypeStruct(cover.shape, f32) for cover in covers],
         ],
         compiler_params=pltpu.CompilerParams(vmem_limit_bytes=VMEM_LIMIT),
         cost_estimate=pl.CostEstimate(
@@ -292,7 +299,7 @@
             bytes_accessed=8 * slots * width * width,
             transcendentals=2 * slots * width * width,
         ),
-    )(up_at, down_at, counts, place, x, h, up_weight, down_weight, f_cover, u_cover)
+    )(up_at, down_at, counts, place, x, h, up_weight, down_weight, *covers)
 
 
 def silu_pair(hidden):
@@ -463,16 +470,23 @@
 
 def final_kernel(
     sums_ref,
-    f_ref,
-    u_ref,
-    out_ref,
-    f_out,
-    u_out,
+    up_rows,
+    up_cols,
+    down_rows,
+    down_cols,
+    mixed_ref,
+    grad_ref,
+    up_rows_out,
+    up_cols_out,
+    down_rows_out,
+    down_cols_out,
     from_dp,
     to_row,
     from_row,
     f_dp,
     u_dp,
+    f_own,
+    u_own,
     f_row,
     u_col,
     dp_send,
@@ -500,9 +514,13 @@
         )
         for k, target in enumerate(targets)
     ]
+    f_own[0] = up_rows[...]
+    f_own[1] = down_cols[...]
+    u_own[0] = up_cols[...]
+    u_own[1] = down_rows[...]
     max_copies = [
-        send(f_ref, f_dp, max_send.at[0], max_recv.at[0], partner),
-        send(u_ref, u_dp, max_send.at[1], max_recv.at[1], partner),
+        send(f_own, f_dp, max_send.at[0], max_recv.at[0], partner),
+        send(u_own, u_dp, max_send.at[1], max_recv.at[1], partner),
     ]
     row_copies = []
     for k, target in enumerate(targets):
@@ -516,58 +534,65 @@
             )
     max_copies[0].wait_recv()
     max_copies[0].wait_send()
-    f_out[...] = jnp.maximum(f_ref[...], f_dp[...])
+    f_own[...] = jnp.maximum(f_own[...], f_dp[...])
     max_copies[1].wait_recv()
     max_copies[1].wait_send()
-    u_out[...] = jnp.maximum(u_ref[...], u_dp[...])
-    f_own = f_out[...]
-    f_dp[...] = f_own
-    u_own = u_out[...]
-    u_dp[...] = u_own
+    u_own[...] = jnp.maximum(u_own[...], u_dp[...])
     f_copies = [
-        send(f_dp, f_row.at[k], f_send.at[k], f_recv.at[k], peer) for k, peer in enumerate(peers)
+        send(f_own, f_row.at[k], f_send.at[k], f_recv.at[k], peer) for k, peer in enumerate(peers)
     ]
     u_copies = [
-        send(u_dp, u_col.at[k], u_send.at[k], u_recv.at[k], peer) for k, peer in enumerate(columns)
+        send(u_own, u_col.at[k], u_send.at[k], u_recv.at[k], peer) for k, peer in enumerate(columns)
     ]
+    best = u_own[...]
     for k, copy in enumerate(u_copies):
         copy.wait_recv()
-        u_own = jnp.maximum(u_own, u_col[k])
-    u_out[...] = u_own
+        best = jnp.maximum(best, u_col[k])
+    up_cols_out[...] = best[0]
+    down_rows_out[...] = best[1]
     for k, copy in enumerate(row_copies):
         copy.wait_recv()
         total = total + from_row[k].astype(jnp.float32)
-    out_ref[...] = total.astype(jnp.bfloat16)
+    half = mixed_ref.shape[0]
+    mixed_ref[...] = total[:half].astype(jnp.bfloat16)
+    grad_ref[...] = total[half:].astype(jnp.bfloat16)
+    best = f_own[...]
     for k, copy in enumerate(f_copies):
         copy.wait_recv()
-        f_own = jnp.maximum(f_own, f_row[k])
-    f_out[...] = f_own
+        best = jnp.maximum(best, f_row[k])
+    up_rows_out[...] = best[0]
+    down_cols_out[...] = best[1]
     for copy in dp_copies + row_copies + f_copies + u_copies:
         copy.wait_send()
 
 
-def final_exchange(sums, f_new, u_new):
+def final_exchange(sums, *largest):
     size, columns = lax.axis_size("row"), lax.axis_size("col")
     dma = pltpu.SemaphoreType.DMA
     f32, bf16 = jnp.float32, jnp.bfloat16
     piece = sums.shape[1:]
+    f_shape = (2,) + largest[0].shape
+    u_shape = (2,) + largest[1].shape
+    half = jax.ShapeDtypeStruct((piece[0] // 2, piece[1]), bf16)
     return comm_call(
         final_kernel,
         "final_exchange",
         2,
         (
-            jax.ShapeDtypeStruct(piece, bf16),
-            jax.ShapeDtypeStruct(f_new.shape, f32),
-            jax.ShapeDtypeStruct(u_new.shape, f32),
+            half,
+            half,
+            *[jax.ShapeDtypeStruct(value.shape, f32) for value in largest],
         ),
         [
             pltpu.VMEM((size,) + piece, bf16),
             pltpu.VMEM((size - 1,) + piece, bf16),
             pltpu.VMEM((size - 1,) + piece, bf16),
-            pltpu.VMEM(f_new.shape, f32),
-            pltpu.VMEM(u_new.shape, f32),
-            pltpu.VMEM((size - 1,) + f_new.shape, f32),
-            pltpu.VMEM((columns - 1,) + u_new.shape, f32),
+            pltpu.VMEM(f_shape, f32),
+            pltpu.VMEM(u_shape, f32),
+            pltpu.VMEM(f_shape, f32),
+            pltpu.VMEM(u_shape, f32),
+            pltpu.VMEM((size - 1,) + f_shape, f32),
+            pltpu.VMEM((columns - 1,) + u_shape, f32),
             dma((size,)),
             dma((size,)),
             dma((size - 1,)),
@@ -579,7 +604,7 @@
             dma((columns - 1,)),
             dma((columns - 1,)),
         ],
-        (sums, f_new, u_new),
+        (sums, *largest),
     )
 
 
@@ -614,25 +639,27 @@
     own = jnp.stack([tokens, cotangent]).reshape(2 * own_tokens * features, width)
     gathered = gather_inputs(own).reshape(shares * rows, 2, own_tokens, features, width)
     x = gathered.transpose(1, 3, 0, 2, 4).reshape(2, features, all_tokens, width)
-    x = jnp.pad(x, ((0, 0), (0, 1), (0, 0), (0, 0)))
 
     partial = first_products(
         up_at, down_at, counts, place, x, up_weight, down_weight, units, shares
     )
     h = hidden_exchange(partial)
 
-    f_cover = jnp.stack([up_cover_rows, down_cover_cols]).reshape(2, features, width)
-    u_cover = jnp.stack([up_cover_cols, down_cover_rows]).reshape(2, units, width)
-    up_step, down_step, sums, f_new, u_new = second_products(
-        up_at, down_at, counts, place, x, h, up_weight, down_weight, f_cover, u_cover, shares
+    covers = [
+        up_cover_rows.reshape(features, width),
+        up_cover_cols.reshape(units, width),
+        down_cover_rows.reshape(units, width),
+        down_cover_cols.reshape(features, width),
+    ]
+    up_step, down_step, sums, *largest = second_products(
+        up_at, down_at, counts, place, x, h, up_weight, down_weight, covers, shares
     )
     sums = sums.reshape(2, features, shares * rows, own_tokens, width).transpose(2, 0, 3, 1, 4)
     sums = sums.reshape(shares * rows, 2 * own_tokens * features, width)
-    out, f_new, u_new = final_exchange(sums, f_new, u_new)
-    out = out.reshape(2, own_tokens, features * width)
-    f_new = f_new.reshape(2, features * width)
-    u_new = u_new.reshape(2, units * width)
-    return (out[0], out[1], up_step, down_step, f_new[0], u_new[0], u_new[1], f_new[1])
+    mixed, token_grad, *largest = final_exchange(sums, *largest)
+    mixed = mixed.reshape(own_tokens, features * width)
+    token_grad = token_grad.reshape(own_tokens, features * width)
+    return (mixed, token_grad, up_step, down_step, *[value.reshape(-1) for value in largest])
 
 
 def solution(mesh):

time: 124 us -> 104 us (0.84)
  Pallas kernels: 107 us -> 85.1 us
  local copies, waits for them, and re-layouts: 12.5 us -> 15.7 us
  other arithmetic: 3.5 us -> 0.79 us
    pallas_call x1, Pallas kernels: 47 us -> 29.8 us  [second_products(): pl.pallas_call(functools.partial(second_kernel, chunk, batch), grid_spec=...]
    unnamed x2 -> x6, local copies, waits for them, and re-layouts: 1.67 us -> 6.97 us
    pallas_call x1, Pallas kernels: 17.6 us -> 13.5 us  [first_products(): pl.pallas_call(functools.partial(first_kernel, chunk, batch), grid_spec=p...]
    squeeze x4 -> x0, local copies, waits for them, and re-layouts: 3.95 us -> none  [the longest x1 1.37 us: on_device(): u_new[1]]
    reshape x0 -> x2, local copies, waits for them, and re-layouts: none -> 2.72 us  [the longest x1 1.36 us: on_device(): mixed = mixed.reshape(own_tokens, features * width)]
    another operation x2 -> x0, other arithmetic: 2.7 us -> none  [the longest x1 1.37 us: on_device(): jnp.stack([up_cover_cols, down_cover_rows]).reshape(2, units, width)]
where the time goes in v3:
time: 104 us; the launch traced here: 102 us
  Pallas kernels  85.1 us (82%)
  local copies, waits for them, and re-layouts  15.7 us (15%)
    pallas_call x3, Pallas kernels, comm_call(): pl.pallas_call(kernel, name=name, out_shape=out_shape, in_specs=[pl.Block...  41.8 us
    pallas_call x1, Pallas kernels, second_products(): pl.pallas_call(functools.partial(second_kernel, chunk, batch), grid_spec=...  29.8 us
    pallas_call x1, Pallas kernels, first_products(): pl.pallas_call(functools.partial(first_kernel, chunk, batch), grid_spec=p...  13.5 us
    unnamed x6, local copies, waits for them, and re-layouts  6.97 us

profile of v3, /device:TPU:0, one launch (start us, length us, event | category | flops | bytes accessed | tf_op | source)
XLA Modules:
  0.0 102.3 jit_solution(11375999624614877446)
XLA Ops:
  0.6 0.8 pad_maximum_fusion
  1.4 0.6 reshape.83.own_ref
  2.1 0.8 copy.21
  2.9 0.8 reshape.79.up_at
  3.7 0.8 copy.22
  4.6 0.8 reshape.80.down_at
  5.4 12.3 %gather_inputs.1 = bf16[8,192,128]{2,1,0:T(8,128)(2,1)} custom-call(bf16[192,128]{1,0:T(8,128)(2,1)} %reshape.83.own_ref), custom_call_target="tpu_custom_call" | custom-call | tf_op jit(solution)/shard_map/gather_inputs/pallas_call | solution.py:337
  17.7 1.9 %copy.23 = bf16[8,2,4,24,128]{4,2,0,3,1:T(4,128)(2,1)} copy(bf16[8,2,4,24,128]{4,3,2,1,0:T(8,128)(2,1)} %bitcast.33) | data formatting | bytes 786432 | tf_op jit(solution)/shard_map/reshape | solution.py:640
  19.6 13.5 %shard_map.170.part_ref = bf16[2,2,48,16,128]{4,3,2,1,0:T(8,128)(2,1)} custom-call(s32[1152]{0:T(1024)} %reshape.79.up_at, s32[1152]{0:T(1024)} %reshape.80.down_at, s32[2]{0:T(128)} %bitcast.45, s32[1]{0:T(128)} %bitcast.1.place, bf16[2,24,32,128]{3,2,1,0:T(8,128)(2,1)} %bitcast.30, bf16[576,128,128]{2,1,0:T(8,128)(2,1)} %bitcast.26, ...), custom_call_target="tpu_custom_call" | custom-call | flops 603979776 | bytes 18874368 | tf_op jit(solution)/shard_map/pallas_call | solution.py:77
  33.1 15.8 %hidden_exchange.1.h_ref = bf16[2,2,48,16,128]{4,3,2,1,0:T(8,128)(2,1)} custom-call(bf16[2,2,48,16,128]{4,3,2,1,0:T(8,128)(2,1)} %shard_map.170.part_ref), custom_call_target="tpu_custom_call" | custom-call | tf_op jit(solution)/shard_map/hidden_exchange/pallas_call | solution.py:337
  48.9 29.8 %shard_map.171 = (bf16[1,1,288,128,128]{4,3,2,1,0:T(8,128)(2,1)}, bf16[1,1,288,128,128]{4,3,2,1,0:T(8,128)(2,1)}, bf16[2,24,32,128]{3,2,1,0:T(8,128)(2,1)}, f32[...) custom-call(s32[1152]{0:T(1024)} %reshape.79.up_at, s32[1152]{0:T(1024)} %reshape.80.down_at, ...), custom_call_target="tpu_custom_call" | custom-call | flops 1207959552 | bytes 37748736 | tf_op jit(solution)/shard_map/pallas_call | solution.py:255
  78.7 1.9 %copy.24 = bf16[2,24,8,4,128]{4,1,3,0,2:T(8,128)(2,1)} copy(bf16[2,24,8,4,128]{4,3,2,1,0:T(4,128)(2,1)} %bitcast.34) | data formatting | bytes 786432 | tf_op jit(solution)/shard_map/reshape | solution.py:657
  80.6 13.7 %final_exchange.1 = (bf16[96,128]{1,0:T(8,128)(2,1)}, bf16[96,128]{1,0:T(8,128)(2,1)}, f32[24,128]{1,0:T(8,128)}, f32[48,128]{1,0:T(8,128)}, f32[48,128]{1,0:T(8,128)}, /*index=5*/f32[24,128]{1,0:T(8,128)}) custom-call(bf16[8,192,128]{2,1,0:T(8,128)(2,1)} %bitcast.32, f32[24,128]{1,0:T(8,128)} %get-tuple-element.22.up_rows, ...), custom_call_target="tpu_custom_call" | custom-call | tf_op jit(solution)/shard_map/final_exchange/pallas_call | solution.py:337
  94.3 1.4 %reshape.94 = bf16[4,3072]{1,0:T(4,128)(2,1)} reshape(bf16[96,128]{1,0:T(8,128)(2,1)} %get-tuple-element.26) | data formatting | bytes 49152 | tf_op jit(solution)/shard_map/reshape | solution.py:660
  95.7 1.4 %reshape.95 = bf16[4,3072]{1,0:T(4,128)(2,1)} reshape(bf16[96,128]{1,0:T(8,128)(2,1)} %get-tuple-element.27) | data formatting | bytes 49152 | tf_op jit(solution)/shard_map/reshape | solution.py:661
  97.0 1.3 %copy.29 = f32[3072]{0:T(1024)} copy(f32[3072]{0:T(1024)} %bitcast.44) | data formatting | bytes 24576
  98.3 1.3 %copy.30 = f32[6144]{0:T(1024)} copy(f32[6144]{0:T(1024)} %bitcast.38) | data formatting | bytes 49152
  99.7 1.3 %copy.31 = f32[6144]{0:T(1024)} copy(f32[6144]{0:T(1024)} %bitcast.37) | data formatting | bytes 49152
  101.0 1.3 %copy.32 = f32[3072]{0:T(1024)} copy(f32[3072]{0:T(1024)} %bitcast.43) | data formatting | bytes 24576

commit v4 on v3

--- a/solution.py
+++ b/solution.py
@@ -23,9 +23,9 @@
 
 def slot_places(index_ref, slot, live, features, units):
     alive = slot < live
-    read = index_ref[2 * slot]
+    read = index_ref[slot]
     feature = jnp.where(alive, read, features)
-    unit = jnp.where(alive, index_ref[2 * slot + 1], units)
+    unit = jnp.where(alive, index_ref[index_ref.shape[0] // 2 + slot], units)
     return read, feature, unit
 
 
@@ -237,7 +237,7 @@
     slots = up_weight.shape[0] // shares
     _, features, tokens, width = x.shape
     units = h.shape[2]
-    chunk = largest_divisor(slots, 24)
+    chunk = largest_divisor(slots, 48)
     batch = chunk
     steps = slots // chunk
     weight = pl.BlockSpec(
@@ -554,8 +554,8 @@
         copy.wait_recv()
         total = total + from_row[k].astype(jnp.float32)
     half = mixed_ref.shape[0]
-    mixed_ref[...] = total[:half].astype(jnp.bfloat16)
-    grad_ref[...] = total[half:].astype(jnp.bfloat16)
+    mixed_ref[...] = total[:half]
+    grad_ref[...] = total[half:]
     best = f_own[...]
     for k, copy in enumerate(f_copies):
         copy.wait_recv()
@@ -573,7 +573,7 @@
     piece = sums.shape[1:]
     f_shape = (2,) + largest[0].shape
     u_shape = (2,) + largest[1].shape
-    half = jax.ShapeDtypeStruct((piece[0] // 2, piece[1]), bf16)
+    half = jax.ShapeDtypeStruct((piece[0] // 2, piece[1]), f32)
     return comm_call(
         final_kernel,
         "final_exchange",
@@ -608,6 +608,30 @@
     )
 
 
+def place_kernel(own_tokens, *refs):
+    count = len(refs) // 2
+    sources, targets = refs[:count], refs[count:]
+    for source, target in zip(sources[:2], targets[:2]):
+        features, width = source.shape[0] // own_tokens, source.shape[1]
+        for f in range(features):
+            rows = source[pl.ds(f, own_tokens, stride=features), :]
+            target[:, pl.ds(f * width, width)] = rows.astype(target.dtype)
+    for source, target in zip(sources[2:], targets[2:]):
+        target[...] = source[...]
+
+
+def place_outputs(own_tokens, mixed, token_grad, *largest):
+    placed = jax.ShapeDtypeStruct((own_tokens, mixed.size // own_tokens), jnp.bfloat16)
+    return pl.pallas_call(
+        functools.partial(place_kernel, own_tokens),
+        name="place_outputs",
+        out_shape=[placed, placed, *[jax.ShapeDtypeStruct(v.shape, v.dtype) for v in largest]],
+        in_specs=[pl.BlockSpec(memory_space=pltpu.VMEM)] * (2 + len(largest)),
+        out_specs=[pl.BlockSpec(memory_space=pltpu.VMEM)] * (2 + len(largest)),
+        compiler_params=pltpu.CompilerParams(vmem_limit_bytes=8 * 1024 * 1024),
+    )(mixed, token_grad, *largest)
+
+
 def on_device(
     tokens,
     cotangent,
@@ -629,8 +653,8 @@
     rows = lax.axis_size("row")
     all_tokens = own_tokens * rows * shares
 
-    up_at = up_index.reshape(-1)
-    down_at = down_index.reshape(-1)
+    up_at = up_index[0, 0].T.reshape(-1)
+    down_at = down_index[0, 0].T.reshape(-1)
     counts = tile_counts.reshape(-1)
     place = lax.axis_index("dp").astype(jnp.int32).reshape(1)
     up_weight = up_blocks.reshape(up_blocks.shape[2:])
@@ -657,8 +681,7 @@
     sums = sums.reshape(2, features, shares * rows, own_tokens, width).transpose(2, 0, 3, 1, 4)
     sums = sums.reshape(shares * rows, 2 * own_tokens * features, width)
     mixed, token_grad, *largest = final_exchange(sums, *largest)
-    mixed = mixed.reshape(own_tokens, features * width)
-    token_grad = token_grad.reshape(own_tokens, features * width)
+    mixed, token_grad, *largest = place_outputs(own_tokens, mixed, token_grad, *largest)
     return (mixed, token_grad, up_step, down_step, *[value.reshape(-1) for value in largest])
 
 

time: 104 us -> 98.5 us (0.947)
  local copies, waits for them, and re-layouts: 15.7 us -> 11.7 us
    unnamed x6 -> x12, local copies, waits for them, and re-layouts: 6.97 us -> 4.48 us
    reshape x4 -> x2, local copies, waits for them, and re-layouts: 4.33 us -> 2.73 us  [the longest x1 1.36 us: on_device(): up_at = up_index[0, 0].T.reshape(-1)]
    pallas_call x1, Pallas kernels: 29.8 us -> 28.5 us  [second_products(): pl.pallas_call(functools.partial(second_kernel, chunk, batch), grid_spec=...]
where the time goes in v4:
time: 98.5 us; the launch traced here: 97.6 us
  Pallas kernels  84.5 us (86%)
  local copies, waits for them, and re-layouts  11.7 us (12%)
    pallas_call x3, Pallas kernels, comm_call(): pl.pallas_call(kernel, name=name, out_shape=out_shape, in_specs=[pl.Block...  41.9 us
    pallas_call x1, Pallas kernels, second_products(): pl.pallas_call(functools.partial(second_kernel, chunk, batch), grid_spec=...  28.5 us
    pallas_call x1, Pallas kernels, first_products(): pl.pallas_call(functools.partial(first_kernel, chunk, batch), grid_spec=p...  13.5 us
    unnamed x12, local copies, waits for them, and re-layouts  4.48 us

profile of v4, /device:TPU:0, one launch (start us, length us, event | category | flops | bytes accessed | tf_op | source)
XLA Modules:
  0.0 97.6 jit_solution(9875233352323594128)
XLA Ops:
  0.6 1.4 %reshape.73.up_at = s32[1152]{0:T(1024)} reshape(s32[2,576]{1,0:T(2,128)} %bitcast.43) | data formatting | bytes 9216 | tf_op jit(solution)/shard_map/reshape | solution.py:656
  2.0 1.4 %reshape.74.down_at = s32[1152]{0:T(1024)} reshape(s32[2,576]{1,0:T(2,128)} %bitcast.44) | data formatting | bytes 9216 | tf_op jit(solution)/shard_map/reshape | solution.py:657
  3.4 0.8 pad_maximum_fusion
  4.2 0.6 reshape.77.own_ref
  4.8 12.3 %gather_inputs.1 = bf16[8,192,128]{2,1,0:T(8,128)(2,1)} custom-call(bf16[192,128]{1,0:T(8,128)(2,1)} %reshape.77.own_ref), custom_call_target="tpu_custom_call" | custom-call | tf_op jit(solution)/shard_map/gather_inputs/pallas_call | solution.py:337
  17.1 1.9 %copy.19 = bf16[8,2,4,24,128]{4,2,0,3,1:T(4,128)(2,1)} copy(bf16[8,2,4,24,128]{4,3,2,1,0:T(8,128)(2,1)} %bitcast.35) | data formatting | bytes 786432 | tf_op jit(solution)/shard_map/reshape | solution.py:664
  19.0 13.5 %shard_map.170.part_ref = bf16[2,2,48,16,128]{4,3,2,1,0:T(8,128)(2,1)} custom-call(s32[1152]{0:T(1024)} %reshape.73.up_at, s32[1152]{0:T(1024)} %reshape.74.down_at, s32[2]{0:T(128)} %bitcast.45, s32[1]{0:T(128)} %bitcast.5.place, bf16[2,24,32,128]{3,2,1,0:T(8,128)(2,1)} %bitcast.32, bf16[576,128,128]{2,1,0:T(8,128)(2,1)} %bitcast.28, ...), custom_call_target="tpu_custom_call" | custom-call | flops 603979776 | bytes 18874368 | tf_op jit(solution)/shard_map/pallas_call | solution.py:77
  32.5 15.9 %hidden_exchange.1.h_ref = bf16[2,2,48,16,128]{4,3,2,1,0:T(8,128)(2,1)} custom-call(bf16[2,2,48,16,128]{4,3,2,1,0:T(8,128)(2,1)} %shard_map.170.part_ref), custom_call_target="tpu_custom_call" | custom-call | tf_op jit(solution)/shard_map/hidden_exchange/pallas_call | solution.py:337
  48.4 28.5 %shard_map.171 = (bf16[1,1,288,128,128]{4,3,2,1,0:T(8,128)(2,1)}, bf16[1,1,288,128,128]{4,3,2,1,0:T(8,128)(2,1)}, bf16[2,24,32,128]{3,2,1,0:T(8,128)(2,1)}, f32[...) custom-call(s32[1152]{0:T(1024)} %reshape.73.up_at, s32[1152]{0:T(1024)} %reshape.74.down_at, ...), custom_call_target="tpu_custom_call" | custom-call | flops 1207959552 | bytes 37748736 | tf_op jit(solution)/shard_map/pallas_call | solution.py:255
  76.8 1.9 %copy.20 = bf16[2,24,8,4,128]{4,1,3,0,2:T(8,128)(2,1)} copy(bf16[2,24,8,4,128]{4,3,2,1,0:T(4,128)(2,1)} %bitcast.36) | data formatting | bytes 786432 | tf_op jit(solution)/shard_map/reshape | solution.py:681
  78.7 13.7 %final_exchange.1 = (f32[96,128]{1,0:T(8,128)}, f32[96,128]{1,0:T(8,128)}, f32[24,128]{1,0:T(8,128)}, f32[48,128]{1,0:T(8,128)}, f32[48,128]{1,0:T(8,128)}, /*index=5*/f32[24,128]{1,0:T(8,128)}) custom-call(bf16[8,192,128]{2,1,0:T(8,128)(2,1)} %bitcast.34, f32[24,128]{1,0:T(8,128)} %get-tuple-element.28.up_rows, f32[48,128]{1,0:T(8,128)} %get-tuple-element.29.up_cols, ...), custom_call_target="tpu_custom_call" | custom-call | tf_op jit(solution)/shard_map/final_exchange/pallas_call | solution.py:337
  92.5 0.0 copy-start
  92.5 0.8 copy-done
  93.3 0.0 copy-start.1
  93.3 0.8 copy-done.1
  94.1 0.0 copy-start.2
  94.1 0.7 copy-done.2
  94.8 0.0 copy-start.3
  94.8 0.7 copy-done.3
  95.5 0.0 copy-start.4
  95.5 0.7 copy-done.4
  96.3 0.0 copy-start.5
  96.3 0.7 copy-done.5
  97.0 0.7 place_outputs.1
Async XLA Ops:
  92.5 0.8 copy-start
  93.3 0.8 copy-start.1
  94.1 0.7 copy-start.2
  94.8 0.7 copy-start.3
  95.5 0.7 copy-start.4
  96.3 0.7 copy-start.5
